TPU v7x, 32 devices: a whole 2x2x4 slice. The times are simulated.
32 devices in a mesh: seq: 16 (over z, x, core), mp: 2 (over y).
Axes of the slice: x: 2, y: 2, z: 4, core: 2. Of those that a mesh axis runs over, the one named last changes fastest.
Arguments:
- tokens: bfloat16 [1, 4096, 1024], P(None, 'seq'), may hold values from -6 to 6
- prompt_embed: bfloat16 [1, 128, 4096], replicated, may hold values from -6 to 6
- out_grad: bfloat16 [1, 4096, 1024], P(None, 'seq'), may hold values from -6 to 6
- norm_self: float32 [1024], replicated, may hold values from 0.25 to 1.75
- w_query: bfloat16 [1024, 1024], P(None, 'mp'), may hold values from -0.1875 to 0.1875
- w_key: bfloat16 [1024, 1024], P(None, 'mp'), may hold values from -0.1875 to 0.1875
- w_value: bfloat16 [1024, 1024], P(None, 'mp'), may hold values from -0.1875 to 0.1875
- w_out: bfloat16 [1024, 1024], P('mp'), may hold values from -0.75 to 0.75
- norm_cross: float32 [1024], replicated, may hold values from 0.25 to 1.75
- c_query: bfloat16 [1024, 1024], P(None, 'mp'), may hold values from -0.1875 to 0.1875
- c_key: bfloat16 [4096, 1024], P(None, 'mp'), may hold values from -0.09375 to 0.09375
- c_value: bfloat16 [4096, 1024], P(None, 'mp'), may hold values from -0.09375 to 0.09375
- c_out: bfloat16 [1024, 1024], P('mp'), may hold values from -0.375 to 0.375
- norm_feed: float32 [1024], replicated, may hold values from 0.25 to 1.75
- w_up: bfloat16 [1024, 4096], P(None, 'mp'), may hold values from -0.1875 to 0.1875
- b_up: float32 [4096], P('mp'), may hold values from -3 to 3
- w_down: bfloat16 [4096, 1024], P('mp'), may hold values from -0.09375 to 0.09375
- b_down: float32 [1024], replicated, may hold values from -3 to 3
- timesteps: int32 [1], replicated, may hold values from 0 to 999
- crop_feats: bfloat16 [1, 256, 256, 256], P(None, 'seq', 'mp'), may hold values from -15 to 15
- crop_grad_in: bfloat16 [1, 256, 256, 256], P(None, 'seq', 'mp'), may hold values from -15 to 15
- crop_gain_one: float32 [256], P('mp'), may hold values from 0.25 to 1.75
- crop_conv_one: bfloat16 [3, 3, 256, 256], P(None, None, None, 'mp'), may hold values from -0.125 to 0.125
- crop_time: bfloat16 [1024, 256], P(None, 'mp'), may hold values from -0.1875 to 0.1875
- crop_gain_two: float32 [256], P('mp'), may hold values from 0.25 to 1.75
- crop_conv_two: bfloat16 [3, 3, 256, 256], P(None, None, 'mp'), may hold values from -0.25 to 0.25
- mid_feats: bfloat16 [1, 128, 256, 128], P(None, 'seq', 'mp'), may hold values from -15 to 15
- mid_grad_in: bfloat16 [1, 128, 256, 128], P(None, 'seq', 'mp'), may hold values from -15 to 15
- mid_gain_one: float32 [256], P('mp'), may hold values from 0.25 to 1.75
- mid_conv_one: bfloat16 [3, 3, 256, 256], P(None, None, None, 'mp'), may hold values from -0.125 to 0.125
- mid_time: bfloat16 [1024, 256], P(None, 'mp'), may hold values from -0.1875 to 0.1875
- mid_gain_two: float32 [256], P('mp'), may hold values from 0.25 to 1.75
- mid_conv_two: bfloat16 [3, 3, 256, 256], P(None, None, 'mp'), may hold values from -0.25 to 0.25
Outputs:
- output: bfloat16 [1, 4096, 1024], P(None, 'seq')
- grad_tokens: float32 [1, 4096, 1024], P(None, 'seq')
- grad_norm_self: float32 [1024], replicated
- grad_query: float32 [1024, 1024], P(None, 'mp')
- grad_key: float32 [1024, 1024], P(None, 'mp')
- grad_value: float32 [1024, 1024], P(None, 'mp')
- grad_out: float32 [1024, 1024], P('mp')
- grad_norm_cross: float32 [1024], replicated
- grad_cquery: float32 [1024, 1024], P(None, 'mp')
- grad_ckey: float32 [4096, 1024], P(None, 'mp')
- grad_cvalue: float32 [4096, 1024], P(None, 'mp')
- grad_cout: float32 [1024, 1024], P('mp')
- grad_norm_feed: float32 [1024], replicated
- grad_up: float32 [1024, 4096], P(None, 'mp')
- grad_up_bias: float32 [4096], P('mp')
- grad_down: float32 [4096, 1024], P('mp')
- grad_down_bias: float32 [1024], replicated
- crop_out: bfloat16 [1, 256, 256, 256], P(None, 'seq', 'mp')
- grad_crop: float32 [1, 256, 256, 256], P(None, 'seq', 'mp')
- grad_crop_gain_one: float32 [256], P('mp')
- grad_crop_conv_one: float32 [3, 3, 256, 256], P(None, None, None, 'mp')
- grad_crop_time: float32 [1024, 256], P(None, 'mp')
- grad_crop_gain_two: float32 [256], P('mp')
- grad_crop_conv_two: float32 [3, 3, 256, 256], P(None, None, 'mp')
- mid_out: bfloat16 [1, 128, 256, 128], P(None, 'seq', 'mp')
- grad_mid: float32 [1, 128, 256, 128], P(None, 'seq', 'mp')
- grad_mid_gain_one: float32 [256], P('mp')
- grad_mid_conv_one: float32 [3, 3, 256, 256], P(None, None, None, 'mp')
- grad_mid_time: float32 [1024, 256], P(None, 'mp')
- grad_mid_gain_two: float32 [256], P('mp')
- grad_mid_conv_two: float32 [3, 3, 256, 256], P(None, None, 'mp')
All inputs are finite; a program needn't handle non-finite values.
Results may differ from a plain program's by a relative error of at most 0.025.
Values may be sent and summed in bfloat16 or wider, within the bound.
A program may use at most 320 MiB of HBM per device.

v0:
```python
from functools import partial
import math

import jax
import jax.numpy as jnp
from jax import lax
from jax.sharding import PartitionSpec as P

D = 1024
HEADS = 16
GROUPS = 32


HIGHEST = lax.Precision.HIGHEST


def as_sent(value):

    def short(part):
        return part.astype(jnp.bfloat16) if part.dtype == jnp.float32 else part

    return jax.tree.map(short, value)


def with_halo(value, sides, width):
    for axis, dim in sides:
        size, length = (lax.axis_size(axis), value.shape[dim])
        up = [(i, (i + 1) % size) for i in range(size - 1)]
        down = [(j, i) for i, j in up]
        last = lax.slice_in_dim(value, length - width, length, axis=dim)
        leading = lax.slice_in_dim(value, 0, width, axis=dim)
        before = lax.ppermute(last, axis, up)
        after = lax.ppermute(leading, axis, down)
        value = jnp.concatenate([before, value, after], axis=dim)
    return value


def layer_norm(values):
    center = values - jnp.mean(values, axis=-1, keepdims=True)
    spread = jnp.mean(center * center, axis=-1, keepdims=True)
    return center * lax.rsqrt(spread + 1e-05)


def norm_scale(values, gain):
    return layer_norm(values) * gain


def project(rows, weight):
    return jnp.einsum("ird,dc->irc", rows, weight, preferred_element_type=jnp.float32)


def project_back(grads, weight):
    return jnp.einsum("irc,dc->ird", grads, weight, preferred_element_type=jnp.float32)


def weight_grad(rows, grads):
    return jnp.einsum("ird,irc->dc", rows, grads, preferred_element_type=jnp.float32)


def sum_heads(partial_sum):
    return lax.psum(partial_sum, "mp")


def attend(query, keys, values, scale):
    scores = jnp.einsum("irhe,ikhe->ihrk", query, keys, preferred_element_type=jnp.float32) * scale
    peak = jnp.max(scores, axis=-1, keepdims=True)
    expo = jnp.exp(scores - peak)
    total = jnp.sum(expo, axis=-1, keepdims=True)
    probs = (expo / total).astype(jnp.bfloat16)
    mixed = jnp.einsum("ihrk,ikhe->irhe", probs, values, preferred_element_type=jnp.float32)
    return (mixed.astype(jnp.bfloat16), peak + jnp.log(total))


def attend_back(query, keys, values, logsum, grad_mixed, scale):
    scores = jnp.einsum("irhe,ikhe->ihrk", query, keys, preferred_element_type=jnp.float32) * scale
    probs = jnp.exp(scores - logsum)
    grad_probs = jnp.einsum(
        "irhe,ikhe->ihrk", grad_mixed, values, preferred_element_type=jnp.float32
    )
    inner = jnp.sum(probs * grad_probs, axis=-1, keepdims=True)
    grad_scores = (probs * (grad_probs - inner)).astype(jnp.bfloat16)
    grad_query = (
        jnp.einsum("ihrk,ikhe->irhe", grad_scores, keys, preferred_element_type=jnp.float32) * scale
    )
    grad_keys = (
        jnp.einsum("ihrk,irhe->ikhe", grad_scores, query, preferred_element_type=jnp.float32)
        * scale
    )
    grad_values = jnp.einsum(
        "ihrk,irhe->ikhe",
        probs.astype(jnp.bfloat16),
        grad_mixed,
        preferred_element_type=jnp.float32,
    )
    return (grad_query, grad_keys, grad_values)


def time_features(steps, width):
    half = width // 2
    freqs = jnp.exp(-math.log(10000.0) * jnp.arange(half, dtype=jnp.float32) / half)
    angles = steps.astype(jnp.float32)[:, None] * freqs[None, :]
    return jax.nn.silu(jnp.concatenate([jnp.cos(angles), jnp.sin(angles)], axis=1))


def group_stats(first, second):
    return lax.psum((first, second), "seq")


def gather_channels(values):
    return lax.all_gather(values, "mp", axis=2, tiled=True)


def sum_channels(values):
    return jax.tree.map(
        lambda part: part.astype(jnp.float32),
        lax.psum_scatter(as_sent(values), "mp", scatter_dimension=2, tiled=True),
    )


def group_forward(values, gain, per_group, count):
    images, rows, chans, cols = values.shape
    grouped = values.reshape(images, rows, chans // per_group, per_group, cols)
    total, squares = group_stats(
        jnp.sum(grouped, axis=(1, 3, 4)), jnp.sum(grouped * grouped, axis=(1, 3, 4))
    )
    mean = total / count
    inverse = lax.rsqrt(squares / count - mean * mean + 1e-05)
    normed = ((grouped - mean[:, None, :, None, None]) * inverse[:, None, :, None, None]).reshape(
        values.shape
    )
    return (normed, inverse, normed * gain[None, None, :, None])


def group_backward(grad_scaled, normed, inverse, gain, per_group, count):
    images, rows, chans, cols = normed.shape
    gain_grad = jnp.sum(grad_scaled * normed, axis=(0, 1, 3))
    shaped = (images, rows, chans // per_group, per_group, cols)
    weighted = (grad_scaled * gain[None, None, :, None]).reshape(shaped)
    normed_groups = normed.reshape(shaped)
    first, second = group_stats(
        jnp.sum(weighted, axis=(1, 3, 4)), jnp.sum(weighted * normed_groups, axis=(1, 3, 4))
    )
    result = inverse[:, None, :, None, None] * (
        weighted
        - first[:, None, :, None, None] / count
        - normed_groups * second[:, None, :, None, None] / count
    )
    return (result.reshape(normed.shape), gain_grad)


def conv_rows(acts, weight):
    padded = with_halo(acts, (("seq", 1),), 1)
    result = lax.conv_general_dilated(
        padded,
        weight,
        (1, 1),
        ((0, 0), (1, 1)),
        dimension_numbers=("NHCW", "HWIO", "NHCW"),
        preferred_element_type=jnp.float32,
    )
    return (result, padded)


def conv_input(grads, weight):
    flipped = jnp.flip(weight, (0, 1)).transpose(0, 1, 3, 2)
    result, padded = conv_rows(grads, flipped)
    return result


def conv_weight(padded, grads):
    rows = grads.shape[1]
    cols = grads.shape[3]
    wide = jnp.pad(padded, ((0, 0), (0, 0), (0, 0), (1, 1)))
    taps = []
    for row_tap in range(3):
        line = []
        for col_tap in range(3):
            window = wide[:, row_tap : row_tap + rows, :, col_tap : col_tap + cols]
            line.append(
                jnp.einsum("irsw,irow->so", window, grads, preferred_element_type=jnp.float32)
            )
        taps.append(jnp.stack(line))
    return jnp.stack(taps)


def res_block(feats, cotangent, features, gain_one, conv_one, time_weight, gain_two, conv_two):
    per_group = conv_one.shape[2] // GROUPS
    count = feats.shape[1] * lax.axis_size("seq") * feats.shape[3] * per_group
    inputs = feats.astype(jnp.float32)
    normed_one, inverse_one, scaled_one = group_forward(inputs, gain_one, per_group, count)
    act_one, silu_one = jax.vjp(jax.nn.silu, scaled_one)
    act_full = gather_channels(act_one.astype(jnp.bfloat16))
    conv_out, padded_one = conv_rows(act_full, conv_one)
    time_full = time_weight.astype(jnp.float32)
    shift = jnp.dot(features, time_full, precision=HIGHEST)
    hidden = conv_out + shift[:, None, :, None]
    normed_two, inverse_two, scaled_two = group_forward(hidden, gain_two, per_group, count)
    act_two, silu_two = jax.vjp(jax.nn.silu, scaled_two)
    partial_two, padded_two = conv_rows(act_two.astype(jnp.bfloat16), conv_two)
    result = inputs + sum_channels(partial_two)
    grad_result = cotangent.astype(jnp.float32)
    grad_branch = gather_channels(cotangent)
    grad_conv_two = conv_weight(padded_two, grad_branch)
    grad_act_two = conv_input(grad_branch, conv_two)
    grad_scaled_two = silu_two(grad_act_two)[0]
    grad_hidden, grad_gain_two = group_backward(
        grad_scaled_two, normed_two, inverse_two, gain_two, per_group, count
    )
    grad_time = jnp.dot(features.T, jnp.sum(grad_hidden, axis=(1, 3)), precision=HIGHEST)
    grad_conv_low = grad_hidden.astype(jnp.bfloat16)
    grad_conv_one = conv_weight(padded_one, grad_conv_low)
    grad_act_one = sum_channels(conv_input(grad_conv_low, conv_one))
    grad_scaled_one = silu_one(grad_act_one)[0]
    grad_input, grad_gain_one = group_backward(
        grad_scaled_one, normed_one, inverse_one, gain_one, per_group, count
    )
    return (
        result.astype(jnp.bfloat16),
        grad_result + grad_input,
        (grad_gain_one, grad_conv_one, grad_time, grad_gain_two, grad_conv_two),
    )


def on_device(
    tokens,
    prompt_embed,
    out_grad,
    norm_self,
    w_query,
    w_key,
    w_value,
    w_out,
    norm_cross,
    c_query,
    c_key,
    c_value,
    c_out,
    norm_feed,
    w_up,
    b_up,
    w_down,
    b_down,
    timesteps,
    crop_feats,
    crop_grad_in,
    crop_gain_one,
    crop_conv_one,
    crop_time,
    crop_gain_two,
    crop_conv_two,
    mid_feats,
    mid_grad_in,
    mid_gain_one,
    mid_conv_one,
    mid_time,
    mid_gain_two,
    mid_conv_two,
):
    head_dim = D // HEADS
    scale = head_dim ** (-0.5)
    local_heads = w_query.shape[1] // head_dim

    def to_heads(values):
        return values.reshape(values.shape[0], values.shape[1], local_heads, head_dim)

    def from_heads(values):
        return values.reshape(values.shape[0], values.shape[1], local_heads * head_dim)

    inputs = tokens.astype(jnp.float32)
    normed_one, back_one = jax.vjp(norm_scale, inputs, norm_self)
    first = normed_one.astype(jnp.bfloat16)
    query = project(first, w_query).astype(jnp.bfloat16)
    keys = project(first, w_key).astype(jnp.bfloat16)
    values = project(first, w_value).astype(jnp.bfloat16)
    keys_all, values_all = (
        lax.all_gather(keys, "seq", axis=1, tiled=True),
        lax.all_gather(values, "seq", axis=1, tiled=True),
    )
    mixed, logsum = attend(to_heads(query), to_heads(keys_all), to_heads(values_all), scale)
    mixed = from_heads(mixed)
    after_one = inputs + sum_heads(project(mixed, w_out))
    normed_two, back_two = jax.vjp(norm_scale, after_one, norm_cross)
    second = normed_two.astype(jnp.bfloat16)
    query_two = project(second, c_query).astype(jnp.bfloat16)
    keys_two = project(prompt_embed, c_key).astype(jnp.bfloat16)
    values_two = project(prompt_embed, c_value).astype(jnp.bfloat16)
    mixed_two, logsum_two = attend(
        to_heads(query_two), to_heads(keys_two), to_heads(values_two), scale
    )
    mixed_two = from_heads(mixed_two)
    after_two = after_one + sum_heads(project(mixed_two, c_out))
    normed_three, back_three = jax.vjp(norm_scale, after_two, norm_feed)
    third = normed_three.astype(jnp.bfloat16)
    hidden = project(third, w_up) + b_up
    units_full, gelu_back = jax.vjp(partial(jax.nn.gelu, approximate=False), hidden)
    units = units_full.astype(jnp.bfloat16)
    output = after_two + sum_heads(project(units, w_down)) + b_down
    grad_final = out_grad.astype(jnp.float32)
    grad_down_bias = jnp.sum(grad_final, axis=(0, 1))
    grad_down = weight_grad(units, out_grad)
    grad_hidden = gelu_back(project_back(out_grad, w_down))[0].astype(jnp.bfloat16)
    grad_up_bias = jnp.sum(grad_hidden.astype(jnp.float32), axis=(0, 1))
    grad_up = weight_grad(third, grad_hidden)
    grad_third = sum_heads(project_back(grad_hidden, w_up))
    grad_into_two, grad_norm_feed = back_three(grad_third)
    grad_after_two = grad_final + grad_into_two
    grad_branch_two = grad_after_two.astype(jnp.bfloat16)
    grad_cout = weight_grad(mixed_two, grad_branch_two)
    grad_mixed_two = project_back(grad_branch_two, c_out).astype(jnp.bfloat16)
    grad_qtwo, grad_ktwo, grad_vtwo = attend_back(
        to_heads(query_two),
        to_heads(keys_two),
        to_heads(values_two),
        logsum_two,
        to_heads(grad_mixed_two),
        scale,
    )
    grad_qtwo = from_heads(grad_qtwo).astype(jnp.bfloat16)
    grad_cquery = weight_grad(second, grad_qtwo)
    text_grads = jnp.concatenate([from_heads(grad_ktwo), from_heads(grad_vtwo)], axis=2)
    text_high = text_grads.astype(jnp.bfloat16)
    text_rest = (text_grads - text_high.astype(jnp.float32)).astype(jnp.bfloat16)
    text_weights = weight_grad(prompt_embed, text_high) + weight_grad(prompt_embed, text_rest)
    local_width = grad_ktwo.shape[2] * grad_ktwo.shape[3]
    grad_ckey = text_weights[:, :local_width]
    grad_cvalue = text_weights[:, local_width:]
    grad_second = sum_heads(project_back(grad_qtwo, c_query))
    grad_into_one, grad_norm_cross = back_two(grad_second)
    grad_after_one = grad_after_two + grad_into_one
    grad_branch_one = grad_after_one.astype(jnp.bfloat16)
    grad_out = weight_grad(mixed, grad_branch_one)
    grad_mixed = project_back(grad_branch_one, w_out).astype(jnp.bfloat16)
    grad_q, key_terms, value_terms = attend_back(
        to_heads(query),
        to_heads(keys_all),
        to_heads(values_all),
        logsum,
        to_heads(grad_mixed),
        scale,
    )
    grad_k, grad_v = (
        lax.psum_scatter(
            from_heads(key_terms).astype(jnp.bfloat16), "seq", scatter_dimension=1, tiled=True
        ).astype(jnp.float32),
        lax.psum_scatter(
            from_heads(value_terms).astype(jnp.bfloat16), "seq", scatter_dimension=1, tiled=True
        ).astype(jnp.float32),
    )
    grad_q = from_heads(grad_q).astype(jnp.bfloat16)
    grad_k = grad_k.astype(jnp.bfloat16)
    grad_v = grad_v.astype(jnp.bfloat16)
    grad_query = weight_grad(first, grad_q)
    grad_key = weight_grad(first, grad_k)
    grad_value = weight_grad(first, grad_v)
    grad_first_part = (
        project_back(grad_q, w_query) + project_back(grad_k, w_key) + project_back(grad_v, w_value)
    )
    grad_first = sum_heads(grad_first_part)
    grad_into_zero, grad_norm_self = back_one(grad_first)
    grad_tokens = grad_after_one + grad_into_zero
    features = time_features(timesteps, crop_time.shape[0])
    crop_out, grad_crop, crop_set = res_block(
        crop_feats,
        crop_grad_in,
        features,
        crop_gain_one,
        crop_conv_one,
        crop_time,
        crop_gain_two,
        crop_conv_two,
    )
    mid_out, grad_mid, mid_set = res_block(
        mid_feats,
        mid_grad_in,
        features,
        mid_gain_one,
        mid_conv_one,
        mid_time,
        mid_gain_two,
        mid_conv_two,
    )
    crop_gone, crop_cone, crop_tgrad, crop_gtwo, crop_ctwo = crop_set
    mid_gone, mid_cone, mid_tgrad, mid_gtwo, mid_ctwo = mid_set
    summed = (
        lax.psum(grad_norm_self.astype(jnp.bfloat16), "seq").astype(jnp.float32),
        lax.psum(grad_query.astype(jnp.bfloat16), "seq").astype(jnp.float32),
        lax.psum(grad_key.astype(jnp.bfloat16), "seq").astype(jnp.float32),
        lax.psum(grad_value.astype(jnp.bfloat16), "seq").astype(jnp.float32),
        lax.psum(grad_out.astype(jnp.bfloat16), "seq").astype(jnp.float32),
        lax.psum(grad_norm_cross.astype(jnp.bfloat16), "seq").astype(jnp.float32),
        lax.psum(grad_cquery.astype(jnp.bfloat16), "seq").astype(jnp.float32),
        lax.psum(grad_ckey.astype(jnp.bfloat16), "seq").astype(jnp.float32),
        lax.psum(grad_cvalue.astype(jnp.bfloat16), "seq").astype(jnp.float32),
        lax.psum(grad_cout.astype(jnp.bfloat16), "seq").astype(jnp.float32),
        lax.psum(grad_norm_feed.astype(jnp.bfloat16), "seq").astype(jnp.float32),
        lax.psum(grad_up.astype(jnp.bfloat16), "seq").astype(jnp.float32),
        lax.psum(grad_up_bias.astype(jnp.bfloat16), "seq").astype(jnp.float32),
        lax.psum(grad_down.astype(jnp.bfloat16), "seq").astype(jnp.float32),
        lax.psum(grad_down_bias.astype(jnp.bfloat16), "seq").astype(jnp.float32),
        lax.psum(crop_gone.astype(jnp.bfloat16), "seq").astype(jnp.float32),
        lax.psum(crop_cone.astype(jnp.bfloat16), "seq").astype(jnp.float32),
        lax.psum(crop_tgrad.astype(jnp.bfloat16), "seq").astype(jnp.float32),
        lax.psum(crop_gtwo.astype(jnp.bfloat16), "seq").astype(jnp.float32),
        lax.psum(crop_ctwo.astype(jnp.bfloat16), "seq").astype(jnp.float32),
        lax.psum(mid_gone.astype(jnp.bfloat16), "seq").astype(jnp.float32),
        lax.psum(mid_cone.astype(jnp.bfloat16), "seq").astype(jnp.float32),
        lax.psum(mid_tgrad.astype(jnp.bfloat16), "seq").astype(jnp.float32),
        lax.psum(mid_gtwo.astype(jnp.bfloat16), "seq").astype(jnp.float32),
        lax.psum(mid_ctwo.astype(jnp.bfloat16), "seq").astype(jnp.float32),
    )
    return (
        output.astype(jnp.bfloat16),
        grad_tokens,
        summed[0],
        summed[1],
        summed[2],
        summed[3],
        summed[4],
        summed[5],
        summed[6],
        summed[7],
        summed[8],
        summed[9],
        summed[10],
        summed[11],
        summed[12],
        summed[13],
        summed[14],
        crop_out,
        grad_crop,
        summed[15],
        summed[16],
        summed[17],
        summed[18],
        summed[19],
        mid_out,
        grad_mid,
        summed[20],
        summed[21],
        summed[22],
        summed[23],
        summed[24],
    )


def solution(mesh):
    in_specs = (
        P(None, "seq", None),
        P(),
        P(None, "seq", None),
        P(),
        P(None, "mp"),
        P(None, "mp"),
        P(None, "mp"),
        P("mp", None),
        P(),
        P(None, "mp"),
        P(None, "mp"),
        P(None, "mp"),
        P("mp", None),
        P(),
        P(None, "mp"),
        P("mp"),
        P("mp", None),
        P(),
        P(),
        P(None, "seq", "mp", None),
        P(None, "seq", "mp", None),
        P("mp"),
        P(None, None, None, "mp"),
        P(None, "mp"),
        P("mp"),
        P(None, None, "mp", None),
        P(None, "seq", "mp", None),
        P(None, "seq", "mp", None),
        P("mp"),
        P(None, None, None, "mp"),
        P(None, "mp"),
        P("mp"),
        P(None, None, "mp", None),
    )
    out_specs = (
        P(None, "seq", None),
        P(None, "seq", None),
        P(),
        P(None, "mp"),
        P(None, "mp"),
        P(None, "mp"),
        P("mp", None),
        P(),
        P(None, "mp"),
        P(None, "mp"),
        P(None, "mp"),
        P("mp", None),
        P(),
        P(None, "mp"),
        P("mp"),
        P("mp", None),
        P(),
        P(None, "seq", "mp", None),
        P(None, "seq", "mp", None),
        P("mp"),
        P(None, None, None, "mp"),
        P(None, "mp"),
        P("mp"),
        P(None, None, "mp", None),
        P(None, "seq", "mp", None),
        P(None, "seq", "mp", None),
        P("mp"),
        P(None, None, None, "mp"),
        P(None, "mp"),
        P("mp"),
        P(None, None, "mp", None),
    )
    return jax.shard_map(
        on_device, mesh=mesh, in_specs=in_specs, out_specs=out_specs, check_vma=False
    )
```

profile of v0, /device:TPU:0, one launch (start us, length us, event | category | flops | bytes accessed | tf_op | source)
XLA Modules:
  0.0 1419.5 jit_solution(12600442022879191749)
XLA Ops:
  15.9 50.1 %all-gather.13.cloned.1.call-done = bf16[4096,512]{1,0:T(8,128)(2,1)} async-done(((bf16[256,512]{1,0:T(8,128)(2,1)}), bf16[4096,512]{1,0:T(8,128)(2,1)}) %all-gather.13.cloned.1.call-update) | async-done | bytes 4194320 | tf_op jit(solution)/shard_map/all_gather | solution.py:276
  66.0 6.3 copy.88
  72.3 15.6 %multiply_reduce_fusion.1 = (f32[8,256]{1,0:T(8,128)S(1)}, f32[8,256,4096]{2,1,0:T(8,128)}) fusion(bf16[256,8,64]{0,2,1:T(8,128)(2,1)S(1)} %bitcast.956, bf16[4096,8,64]{0,2,1:T(8,128)(2,1)} %bitcast.936), kind=kOutput, calls=%fused_computation.6 | convolution fusion | flops 1090516992 | bytes 38019072 | tf_op jit(solution)/shard_map/irhe,ikhe->ihrk/dot_general | solution.py:65
  87.9 14.2 %fusion = f32[8,256]{1,0:T(8,128)S(1)} fusion(f32[8,256,4096]{2,1,0:T(8,128)} %get-tuple-element.217, f32[8,256]{1,0:T(8,128)S(1)} %get-tuple-element.216), kind=kLoop, calls=%fused_computation.5 | loop fusion | flops 25163776 | bytes 33570816 | tf_op jit(solution)/shard_map/reduce_sum | solution.py:68
  102.1 15.7 %all-gather.11.cloned.1.call-done = bf16[4096,512]{1,0:T(8,128)(2,1)} async-done(((bf16[256,512]{1,0:T(8,128)(2,1)}), bf16[4096,512]{1,0:T(8,128)(2,1)}) %all-gather.11.cloned.1.call-update) | async-done | bytes 4194320 | tf_op jit(solution)/shard_map/all_gather | solution.py:277
  124.2 15.7 %fusion.132 = bf16[8,64,256]{2,1,0:T(8,128)(2,1)S(1)} fusion(bf16[4096,8,64]{0,2,1:T(8,128)(2,1)} %bitcast.940, f32[8,256,4096]{2,1,0:T(8,128)} %get-tuple-element.217, f32[8,256]{1,0:T(8,128)S(1)} %fusion, f32[8,256]{1,0:T(8,128)S(1)} %get-tuple-element.216), kind=kOutput, calls=%fused_computation.216 | convolution fusion | flops 1107427328 | bytes 38027264 | tf_op jit(solution)/shard_map/ihrk,ikhe->irhe/dot_general | solution.py:70
  148.0 32.1 %all-reduce.18.cloned.1.call-done = f32[1,256,1024]{2,1,0:T(8,128)} async-done(((f32[1,256,1024]{2,1,0:T(8,128)}), f32[1,256,1024]{2,1,0:T(8,128)}) %all-reduce.18.cloned.1.call-update) | async-done | bytes 1048592 | tf_op jit(solution)/shard_map/psum | solution.py:61
  188.4 40.1 %all-reduce.20.cloned.1.call-done = f32[1,256,1024]{2,1,0:T(8,128)} async-done(((f32[1,256,1024]{2,1,0:T(8,128)}), f32[1,256,1024]{2,1,0:T(8,128)}) %all-reduce.20.cloned.1.call-update) | async-done | bytes 1048592 | tf_op jit(solution)/shard_map/psum | solution.py:61
  231.1 6.8 multiply_convert_fusion.3
  244.3 39.7 %all-reduce.22.cloned.1.call-done = f32[1,256,1024]{2,1,0:T(8,128)} async-done(((f32[1,256,1024]{2,1,0:T(8,128)}), f32[1,256,1024]{2,1,0:T(8,128)}) %all-reduce.22.cloned.1.call-update) | async-done | bytes 1048592 | tf_op jit(solution)/shard_map/psum | solution.py:61
  297.3 33.2 %all-reduce.7 = (f32[1,16]{1,0:T(1,128)S(1)}, f32[1,16]{1,0:T(1,128)S(1)}, f32[1,16]{1,0:T(1,128)S(1)}, f32[1,16]{1,0:T(1,128)S(1)}) all-reduce(f32[1,16]{1,0:T(1,128)S(1)} %bitcast.995, f32[1,16]{1,0:T(1,128)S(1)} %bitcast.996, f32[1,16]{1,0:T(1,128)S(1)} %bitcast.997, ...), channel_id=1, replica_groups=mesh['seq'=16,'mp'=2] {'seq'}, use_global_device_ids=true, to_apply=%region_51.52 | all-reduce | flops 64 | bytes 512 | tf_op jit(solution)/shard_map/psum | solution.py:106
  341.6 24.9 %multiply_reduce_fusion = (f32[8,256]{1,0:T(8,128)S(1)}, f32[8,256,4096]{2,1,0:T(8,128)}) fusion(f32[8,256,4096]{2,1,0:T(8,128)} %get-tuple-element.217, f32[8,256]{1,0:T(8,128)S(1)} %log_add_fusion, bf16[256,8,64]{0,2,1:T(8,128)(2,1)S(1)} %bitcast.954, bf16[4096,8,64]{0,2,1:T(8,128)(2,1)} %bitcast.941), kind=kOutput, calls=%fused_computation.1 | convolution fusion | flops 1107294208 | bytes 71581696 | tf_op jit(solution)/shard_map/irhe,ikhe->ihrk/dot_general | solution.py:77
  366.5 28.2 %multiply_convert_fusion = bf16[8,256,4096]{2,1,0:T(8,128)(2,1)} fusion(f32[8,256,4096]{2,1,0:T(8,128)} %get-tuple-element.224, f32[8,256,4096]{2,1,0:T(8,128)} %get-tuple-element.217, f32[8,256]{1,0:T(8,128)S(1)} %get-tuple-element.223, f32[8,256]{1,0:T(8,128)S(1)} %log_add_fusion), kind=kLoop, calls=%fused_computation | loop fusion | flops 41943040 | bytes 83902464 | tf_op jit(solution)/shard_map/convert_element_type | solution.py:81
  394.7 10.8 multiply_convert_fusion.1
  406.6 8.9 all_gather.22
  418.2 7.5 all_gather.23
  446.0 6.8 collective-permute-start
  476.5 6.8 select_reduce_fusion.5
  483.7 31.5 %all-reduce.6 = (f32[1,16]{1,0:T(1,128)S(1)}, f32[1,16]{1,0:T(1,128)S(1)}, f32[1,16]{1,0:T(1,128)S(1)}, f32[1,16]{1,0:T(1,128)S(1)}) all-reduce(f32[1,16]{1,0:T(1,128)S(1)} %bitcast.998, f32[1,16]{1,0:T(1,128)S(1)} %bitcast.1001, f32[1,16]{1,0:T(1,128)S(1)} %bitcast.991, ...), channel_id=1, replica_groups=mesh['seq'=16,'mp'=2] {'seq'}, use_global_device_ids=true, to_apply=%region_57.58 | all-reduce | flops 64 | bytes 512 | tf_op jit(solution)/shard_map/psum | solution.py:106
  515.2 15.7 %fusion.8 = bf16[8,64,4096]{2,1,0:T(8,128)(2,1)} fusion(bf16[256,8,64]{0,2,1:T(8,128)(2,1)S(1)} %bitcast.955, f32[8,256,4096]{2,1,0:T(8,128)} %get-tuple-element.217, f32[8,256]{1,0:T(8,128)S(1)} %log_add_fusion), kind=kOutput, calls=%fused_computation.15 | convolution fusion | flops 1101004800 | bytes 38019072 | tf_op jit(solution)/shard_map/ihrk,irhe->ikhe/dot_general | solution.py:89
  551.4 8.0 select_reduce_fusion.3
  564.4 30.7 %all-reduce.5 = (f32[16]{0:T(128)S(1)}, f32[1,16]{1,0:T(1,128)S(1)}, f32[16]{0:T(128)S(1)}, f32[1,16]{1,0:T(1,128)S(1)}) all-reduce(f32[16]{0:T(128)S(1)} %reduce_sum.616, f32[1,16]{1,0:T(1,128)S(1)} %bitcast.993, f32[16]{0:T(128)S(1)} %reduce_sum.651, f32[1,16]{1,0:T(1,128)S(1)} %bitcast.1002), channel_id=1, replica_groups=mesh['seq'=16,'mp'=2] {'seq'}, use_global_device_ids=true, to_apply=%region_64.65 | all-reduce | flops 64 | bytes 512 | tf_op jit(solution)/shard_map/psum | solution.py:106
  794.6 8.1 fusion.366
  802.7 11.7 fusion.7
  814.4 12.3 fusion.130
  833.5 7.6 fusion.595
  854.7 29.7 %all-reduce.4 = (f32[16]{0:T(128)S(1)}, f32[1,16]{1,0:T(1,128)S(1)}, f32[16]{0:T(128)S(1)}, f32[1,16]{1,0:T(1,128)S(1)}) all-reduce(f32[16]{0:T(128)S(1)} %reduce_sum.624, f32[1,16]{1,0:T(1,128)S(1)} %bitcast.999, f32[16]{0:T(128)S(1)} %reduce_sum.659, f32[1,16]{1,0:T(1,128)S(1)} %bitcast.994), channel_id=1, replica_groups=mesh['seq'=16,'mp'=2] {'seq'}, use_global_device_ids=true, to_apply=%region_71.72 | all-reduce | flops 64 | bytes 512 | tf_op jit(solution)/shard_map/psum | solution.py:106
  896.8 64.8 %all-reduce.9 = (bf16[1024]{0:T(1024)(128)(2,1)S(1)}, bf16[1024]{0:T(1024)(128)(2,1)S(1)}, bf16[1024]{0:T(1024)(128)(2,1)S(1)}, bf16[2048]{0:T(1024)(128)(2,1)S(...) all-reduce(bf16[1024]{0:T(1024)(128)(2,1)S(1)} %get-tuple-element.1, ...), channel_id=1, replica_groups=mesh['seq'=16,'mp'=2] {'seq'}, use_global_device_ids=true, to_apply=%region_27.0 | all-reduce | flops 6656 | bytes 26624 | tf_op jit(solution)/shard_map/psum | solution.py:385
  970.4 399.6 %all-reduce.28.cloned.1.call-done = (bf16[4096,512]{0,1:T(8,128)(2,1)}, bf16[4096,512]{0,1:T(8,128)(2,1)}, bf16[1024,512]{1,0:T(8,128)(2,1)}, bf16[1024,512]{1,0...) async-done(((bf16[4096,512]{0,1:T(8,128)(2,1)}, ...) | async-done | bytes 25952272 | tf_op jit(solution)/shard_map/psum | solution.py:392
  1379.4 7.0 copy.154
  1386.4 7.1 copy.155
  1395.1 6.8 convert_element_type.504
  (783 shorter events, 397.4 us)
Async XLA Ops:
  7.2 58.8 %all-gather.13.cloned.1.call-start = ((), (), s32[]{:S(2)}) async-start(), calls=%async_computation.19 | async-start | bytes 4456448 | tf_op jit(solution)/shard_map/all_gather | solution.py:276
  12.6 105.3 %all-gather.11.cloned.1.call-start = ((), (), s32[]{:S(2)}) async-start(), calls=%async_computation.18 | async-start | bytes 4456448 | tf_op jit(solution)/shard_map/all_gather | solution.py:277
  15.2 164.9 %all-reduce.18.cloned.1.call-start = ((), (), s32[]{:S(2)}) async-start(), calls=%async_computation.6 | async-start | bytes 2097152 | tf_op jit(solution)/shard_map/psum | solution.py:61
  141.4 87.2 %all-reduce.20.cloned.1.call-start = ((), (), s32[]{:S(2)}) async-start(), calls=%async_computation.7 | async-start | bytes 2097152 | tf_op jit(solution)/shard_map/psum | solution.py:61
  188.4 95.6 %all-reduce.22.cloned.1.call-start = ((), (), s32[]{:S(2)}) async-start(), calls=%async_computation.8 | async-start | bytes 2097152 | tf_op jit(solution)/shard_map/psum | solution.py:61
  243.8 92.3 %all-reduce.24.cloned.1.call-start = ((), (), s32[]{:S(2)}) async-start(), calls=%async_computation.9 | async-start | bytes 2097152 | tf_op jit(solution)/shard_map/psum | solution.py:61
  295.9 148.5 %all-gather.7.cloned.1.call-start = ((), (), s32[]{:S(2)}) async-start(), calls=%async_computation.12 | async-start | bytes 3145728 | tf_op jit(solution)/shard_map/all_gather | solution.py:110
  332.6 121.4 %all-gather.9.cloned.1.call-start = ((), (), s32[]{:S(2)}) async-start(), calls=%async_computation.14 | async-start | bytes 3145728 | tf_op jit(solution)/shard_map/all_gather | solution.py:110
  333.4 494.8 %reduce-scatter.7.cloned.1.call-start = ((), (), s32[]{:S(2)}) async-start(), calls=%async_computation.10 | async-start | bytes 4456448 | tf_op jit(solution)/shard_map/reduce_scatter | solution.py:342
  405.5 424.8 %reduce-scatter.9.cloned.1.call-start = ((), (), s32[]{:S(2)}) async-start(), calls=%async_computation.11 | async-start | bytes 4456448 | tf_op jit(solution)/shard_map/reduce_scatter | solution.py:345
  415.6 18.5 %collective-permute-start.8 = (bf16[1,1,256,128]{3,2,1,0:T(8,128)(2,1)S(1)}, bf16[1,1,256,128]{3,2,1,0:T(8,128)(2,1)S(1)}, u32[]{:S(2)}, u32[]{:S(2)}) collective-permute-start(bf16[1,1,256,128]{3,2,1,0:T(8,128)(2,1)S(1)} %get-tuple-element.197), channel_id=1, source_target_pairs={{0,2},{2,4},{4,6},{6,8},{8,10},{10,12},{12,14},{14,16},{16,18},{18... | collective-permute-start | bytes 196616 | tf_op jit(solution)/shard_map/ppermute | solution.py:32
  416.9 17.3 %collective-permute-start.9 = (bf16[1,1,256,128]{3,2,1,0:T(8,128)(2,1)S(1)}, bf16[1,1,256,128]{3,2,1,0:T(8,128)(2,1)S(1)}, u32[]{:S(2)}, u32[]{:S(2)}) collective-permute-start(bf16[1,1,256,128]{3,2,1,0:T(8,128)(2,1)S(1)} %get-tuple-element.196), channel_id=1, source_target_pairs={{2,0},{4,2},{6,4},{8,6},{10,8},{12,10},{14,12},{16,14},{18,16},{20... | collective-permute-start | bytes 196616 | tf_op jit(solution)/shard_map/ppermute | solution.py:33
  426.4 15.5 %collective-permute-start.13 = (bf16[1,1,256,128]{3,2,1,0:T(8,128)(2,1)}, bf16[1,1,256,128]{3,2,1,0:T(8,128)(2,1)S(1)}, u32[]{:S(2)}, u32[]{:S(2)}) collective-permute-start(bf16[1,1,256,128]{3,2,1,0:T(8,128)(2,1)} %get-tuple-element.195), channel_id=1, source_target_pairs={{2,0},{4,2},{6,4},{8,6},{10,8},{12,10},{14,12},{16,14},{18,16},{20... | collective-permute-start | bytes 196616 | tf_op jit(solution)/shard_map/ppermute | solution.py:33
  427.7 14.2 %collective-permute-start.12 = (bf16[1,1,256,128]{3,2,1,0:T(8,128)(2,1)S(1)}, bf16[1,1,256,128]{3,2,1,0:T(8,128)(2,1)S(1)}, u32[]{:S(2)}, u32[]{:S(2)}) collective-permute-start(bf16[1,1,256,128]{3,2,1,0:T(8,128)(2,1)S(1)} %get-tuple-element.194), channel_id=1, source_target_pairs={{0,2},{2,4},{4,6},{6,8},{8,10},{10,12},{12,14},{14,16},{16,18},{18... | collective-permute-start | bytes 196616 | tf_op jit(solution)/shard_map/ppermute | solution.py:32
  446.0 15.4 %collective-permute-start = (bf16[1,1,256,256]{3,2,1,0:T(8,128)(2,1)S(1)}, bf16[1,1,256,256]{3,2,1,0:T(8,128)(2,1)}, u32[]{:S(2)}, u32[]{:S(2)}) collective-permute-start(bf16[1,1,256,256]{3,2,1,0:T(8,128)(2,1)S(1)} %get-tuple-element.181), channel_id=1, source_target_pairs={{0,2},{2,4},{4,6},{6,8},{8,10},{10,12},{12,14},{14,16},{16,18},{18... | collective-permute-start | bytes 393224 | tf_op jit(solution)/shard_map/ppermute | solution.py:32
  452.7 11.3 collective-permute-start.1
  455.8 76.0 %collective-permute-start.5 = (bf16[1,1,256,256]{3,2,1,0:T(8,128)(2,1)}, bf16[1,1,256,256]{3,2,1,0:T(8,128)(2,1)}, u32[]{:S(2)}, u32[]{:S(2)}) collective-permute-start(bf16[1,1,256,256]{3,2,1,0:T(8,128)(2,1)} %get-tuple-element.183), channel_id=1, source_target_pairs={{2,0},{4,2},{6,4},{8,6},{10,8},{12,10},{14,12},{16,14},{18,16},{20... | collective-permute-start | bytes 393224 | tf_op jit(solution)/shard_map/ppermute | solution.py:33
  457.0 74.7 %collective-permute-start.4 = (bf16[1,1,256,256]{3,2,1,0:T(8,128)(2,1)}, bf16[1,1,256,256]{3,2,1,0:T(8,128)(2,1)}, u32[]{:S(2)}, u32[]{:S(2)}) collective-permute-start(bf16[1,1,256,256]{3,2,1,0:T(8,128)(2,1)} %get-tuple-element.182), channel_id=1, source_target_pairs={{0,2},{2,4},{4,6},{6,8},{8,10},{10,12},{12,14},{14,16},{16,18},{18... | collective-permute-start | bytes 393224 | tf_op jit(solution)/shard_map/ppermute | solution.py:32
  530.9 316.5 %reduce-scatter.17.cloned.1.call-start = ((), (), s32[]{:S(2)}) async-start(), calls=%async_computation.17 | async-start | bytes 786432 | tf_op jit(solution)/shard_map/reduce_scatter | solution.py:116
  601.4 82.7 %collective-permute-start.7 = (bf16[1,1,128,256]{3,2,1,0:T(8,128)(2,1)}, bf16[1,1,128,256]{3,2,1,0:T(8,128)(2,1)}, u32[]{:S(2)}, u32[]{:S(2)}) collective-permute-start(bf16[1,1,128,256]{3,2,1,0:T(8,128)(2,1)} %bitcast.84), channel_id=1, source_target_pairs={{2,0},{4,2},{6,4},{8,6},{10,8},{12,10},{14,12},{16,14},{18,16},{20... | collective-permute-start | bytes 196616 | tf_op jit(solution)/shard_map/ppermute | solution.py:33
  608.3 80.1 %collective-permute-start.6 = (bf16[1,1,128,256]{3,2,1,0:T(8,128)(2,1)}, bf16[1,1,128,256]{3,2,1,0:T(8,128)(2,1)}, u32[]{:S(2)}, u32[]{:S(2)}) collective-permute-start(bf16[1,1,128,256]{3,2,1,0:T(8,128)(2,1)} %bitcast.81), channel_id=1, source_target_pairs={{0,2},{2,4},{4,6},{6,8},{8,10},{10,12},{12,14},{14,16},{16,18},{18... | collective-permute-start | bytes 196616 | tf_op jit(solution)/shard_map/ppermute | solution.py:32
  616.0 36.8 %collective-permute-start.15 = (bf16[1,1,128,128]{3,2,1,0:T(8,128)(2,1)}, bf16[1,1,128,128]{3,2,1,0:T(8,128)(2,1)}, u32[]{:S(2)}, u32[]{:S(2)}) collective-permute-start(bf16[1,1,128,128]{3,2,1,0:T(8,128)(2,1)} %bitcast.181), channel_id=1, source_target_pairs={{2,0},{4,2},{6,4},{8,6},{10,8},{12,10},{14,12},{16,14},{18,16},{20... | collective-permute-start | bytes 98312 | tf_op jit(solution)/shard_map/ppermute | solution.py:33
  620.0 36.8 %collective-permute-start.14 = (bf16[1,1,128,128]{3,2,1,0:T(8,128)(2,1)}, bf16[1,1,128,128]{3,2,1,0:T(8,128)(2,1)}, u32[]{:S(2)}, u32[]{:S(2)}) collective-permute-start(bf16[1,1,128,128]{3,2,1,0:T(8,128)(2,1)} %bitcast.178), channel_id=1, source_target_pairs={{0,2},{2,4},{4,6},{6,8},{8,10},{10,12},{12,14},{14,16},{16,18},{18... | collective-permute-start | bytes 98312 | tf_op jit(solution)/shard_map/ppermute | solution.py:32
  627.4 121.5 %collective-permute-start.3 = (bf16[1,1,128,256]{3,2,1,0:T(8,128)(2,1)}, bf16[1,1,128,256]{3,2,1,0:T(8,128)(2,1)}, u32[]{:S(2)}, u32[]{:S(2)}) collective-permute-start(bf16[1,1,128,256]{3,2,1,0:T(8,128)(2,1)} %bitcast.72), channel_id=1, source_target_pairs={{2,0},{4,2},{6,4},{8,6},{10,8},{12,10},{14,12},{16,14},{18,16},{20... | collective-permute-start | bytes 196616 | tf_op jit(solution)/shard_map/ppermute | solution.py:33
  652.8 96.1 %collective-permute-start.2 = (bf16[1,1,128,256]{3,2,1,0:T(8,128)(2,1)}, bf16[1,1,128,256]{3,2,1,0:T(8,128)(2,1)}, u32[]{:S(2)}, u32[]{:S(2)}) collective-permute-start(bf16[1,1,128,256]{3,2,1,0:T(8,128)(2,1)} %bitcast.990), channel_id=1, source_target_pairs={{0,2},{2,4},{4,6},{6,8},{8,10},{10,12},{12,14},{14,16},{16,18},{18... | collective-permute-start | bytes 196616 | tf_op jit(solution)/shard_map/ppermute | solution.py:32
  656.8 64.6 %collective-permute-start.11 = (bf16[1,1,128,128]{3,2,1,0:T(8,128)(2,1)}, bf16[1,1,128,128]{3,2,1,0:T(8,128)(2,1)}, u32[]{:S(2)}, u32[]{:S(2)}) collective-permute-start(bf16[1,1,128,128]{3,2,1,0:T(8,128)(2,1)} %bitcast.169), channel_id=1, source_target_pairs={{2,0},{4,2},{6,4},{8,6},{10,8},{12,10},{14,12},{16,14},{18,16},{20... | collective-permute-start | bytes 98312 | tf_op jit(solution)/shard_map/ppermute | solution.py:33
  671.5 178.7 %reduce-scatter.13.cloned.1.call-start = ((), (), s32[]{:S(2)}) async-start(), calls=%async_computation.15 | async-start | bytes 3145728 | tf_op jit(solution)/shard_map/reduce_scatter | solution.py:116
  684.2 37.2 %collective-permute-start.10 = (bf16[1,1,128,128]{3,2,1,0:T(8,128)(2,1)}, bf16[1,1,128,128]{3,2,1,0:T(8,128)(2,1)}, u32[]{:S(2)}, u32[]{:S(2)}) collective-permute-start(bf16[1,1,128,128]{3,2,1,0:T(8,128)(2,1)} %bitcast.166), channel_id=1, source_target_pairs={{0,2},{2,4},{4,6},{6,8},{8,10},{10,12},{12,14},{14,16},{16,18},{18... | collective-permute-start | bytes 98312 | tf_op jit(solution)/shard_map/ppermute | solution.py:32
  709.6 175.5 %reduce-scatter.15.cloned.1.call-start = ((), (), s32[]{:S(2)}) async-start(), calls=%async_computation.16 | async-start | bytes 786432 | tf_op jit(solution)/shard_map/reduce_scatter | solution.py:116
  743.0 144.3 %reduce-scatter.11.cloned.1.call-start = ((), (), s32[]{:S(2)}) async-start(), calls=%async_computation.13 | async-start | bytes 3145728 | tf_op jit(solution)/shard_map/reduce_scatter | solution.py:116
  770.4 123.0 %all-reduce.26.cloned.1.call-start = ((), (), s32[]{:S(2)}) async-start(), calls=%async_computation.20 | async-start | bytes 4194304 | tf_op jit(solution)/shard_map/psum | solution.py:61
  833.2 536.8 %all-reduce.28.cloned.1.call-start = ((), (), s32[]{:S(2)}) async-start(), calls=%async_computation.21 | async-start | bytes 51904512 | tf_op jit(solution)/shard_map/psum | solution.py:392
  (179 other events, 1671.9 us)
Sparse Core Ops, SparseCore 0:
  12.7 53.2 all-gather.12
  68.7 49.1 all-gather.10
  141.5 38.5 all-reduce.17
  188.5 40.0 all-reduce.19
  243.9 40.0 all-reduce.21
  296.0 40.0 all-reduce.23
  338.2 33.1 all-gather.6
  372.9 33.1 all-gather.8
  410.5 75.1 reduce-scatter.6
  531.1 69.4 reduce-scatter.8
  671.6 13.7 reduce-scatter.16
  709.7 28.9 reduce-scatter.12
  743.1 12.3 reduce-scatter.14
  770.6 28.8 reduce-scatter.10
  833.3 60.1 all-reduce.25
  903.2 466.8 all-reduce.27
where the time goes:
time: 1430 us; the launch traced here: 1420 us
  waiting for transfers between devices  582 us (41%)
  matrix products  251 us (18%)
  blocking collectives  206 us (14%)
  local copies, waits for them, and re-layouts  177 us (12%)
  other arithmetic  139 us (10%)
  starting transfers between devices  45.9 us (3%)
  between operations  18 us (1%)
    psum x1, waiting for transfers between devices, on_device(): lax.psum(grad_ckey.astype(jnp.bfloat16), 'seq').astype(jnp.float32)  400 us
    psum x4, blocking collectives, group_stats(): return lax.psum((first, second), 'seq')  125 us
    psum x5, waiting for transfers between devices, sum_heads(): return lax.psum(partial_sum, 'mp')  116 us
    unnamed x388, local copies, waits for them, and re-layouts  74.4 us
    psum x1, blocking collectives, on_device(): lax.psum(grad_norm_self.astype(jnp.bfloat16), 'seq').astype(jnp.float32)  64.8 us
    all_gather x1, waiting for transfers between devices, on_device(): lax.all_gather(keys, 'seq', axis=1, tiled=True)  50.1 us
    dot_general x36, matrix products, conv_weight(): jnp.einsum('irsw,irow->so', window, grads, preferred_element_type=jnp.flo...  44.3 us
    dot_general x10, matrix products, weight_grad(): jnp.einsum('ird,irc->dc', rows, grads, preferred_element_type=jnp.float32)  35.7 us
  transfers between devices with their start and end apart: 32, of which 8 were waited for; matrix products, arithmetic and copies ran while one was open for 32% of the time, Pallas kernels for 0%

commit v1 on v0

v1 whole, which is shorter than its diff:
```python
from functools import partial
import math

import jax
import jax.numpy as jnp
from jax import lax
from jax.experimental import pallas as pl
from jax.experimental.pallas import tpu as pltpu
from jax.sharding import PartitionSpec as P

D = 1024
HEADS = 16
GROUPS = 32
E = D // HEADS
SCALE = E ** (-0.5)
COEF = SCALE * math.log2(math.e)
KEY_CHUNK = 512
VMEM_LIMIT = 60 * 1024 * 1024
RINGS = 4

HIGHEST = lax.Precision.HIGHEST
MESH = pl.DeviceIdType.MESH
F32 = jnp.float32
BF16 = jnp.bfloat16


def dot(left, right):
    return jnp.dot(left, right, preferred_element_type=F32)


def dot_nt(left, right):
    return lax.dot_general(left, right, (((1,), (1,)), ((), ())), preferred_element_type=F32)


def dot_tn(left, right):
    return lax.dot_general(left, right, (((0,), (0,)), ((), ())), preferred_element_type=F32)


def wrap(value, size):
    value = jnp.where(value < 0, value + size, value)
    return jnp.where(value >= size, value - size, value)


def turn(block):
    return block.astype(F32).T.astype(BF16)


def greet(peers):
    barrier = pltpu.get_barrier_semaphore()
    for peer in peers:
        pl.semaphore_signal(barrier, inc=1, device_id=peer, device_id_type=MESH)
    pl.semaphore_wait(barrier, len(peers))


def remote(src, dst, send_sem, recv_sem, peer):
    return pltpu.make_async_remote_copy(
        src_ref=src,
        dst_ref=dst,
        send_sem=send_sem,
        recv_sem=recv_sem,
        device_id=peer,
        device_id_type=MESH,
    )


def vmem_call(kernel, outs, scratch, collective_id, name, in_any=(), out_any=(), aliases=None):
    def call(*args):
        return pl.pallas_call(
            kernel,
            out_shape=[jax.ShapeDtypeStruct(shape, kind) for shape, kind in outs],
            in_specs=[
                pl.BlockSpec(memory_space=pl.ANY if i in in_any else pltpu.VMEM)
                for i in range(len(args))
            ],
            out_specs=[
                pl.BlockSpec(memory_space=pl.ANY if i in out_any else pltpu.VMEM)
                for i in range(len(outs))
            ],
            scratch_shapes=scratch,
            input_output_aliases=aliases or {},
            compiler_params=pltpu.CompilerParams(
                collective_id=collective_id,
                has_side_effects=True,
                vmem_limit_bytes=VMEM_LIMIT,
            ),
            name=name,
        )(*args)

    return call


def norm_parts(values):
    center = values - jnp.mean(values, axis=-1, keepdims=True)
    inverse = lax.rsqrt(jnp.mean(center * center, axis=-1, keepdims=True) + 1e-05)
    return center * inverse, inverse


def norm_back(grad, normed, inverse, gain):
    gain_grad = jnp.sum(grad * normed, axis=0, keepdims=True)
    scaled = grad * gain
    first = jnp.mean(scaled, axis=-1, keepdims=True)
    second = jnp.mean(scaled * normed, axis=-1, keepdims=True)
    return inverse * (scaled - first - normed * second), gain_grad


class Exchange:
    def __init__(self, land, send_sem, recv_sem, m):
        self.land, self.send_sem, self.recv_sem, self.m = land, send_sem, recv_sem, m
        self.me = lax.axis_index("mp")

    def peer(self, d):
        return lax.rem(self.me + d, self.m)

    def send(self, key, rows, block):
        self.land[key, self.me, rows, :] = block.astype(BF16)
        for d in range(1, self.m):
            to = self.peer(d)
            part = self.land.at[key, self.me, rows, :]
            remote(
                part, part, self.send_sem.at[key, d], self.recv_sem.at[key, self.me], {"mp": to}
            ).start()

    def wait(self, key, rows):
        for d in range(1, self.m):
            src = self.peer(d)
            part = self.land.at[key, src, rows, :]
            copy = remote(
                part, part, self.send_sem.at[key, d], self.recv_sem.at[key, src], {"mp": src}
            )
            copy.wait_send()
            copy.wait_recv()
        total = self.land[key, 0, rows, :].astype(F32)
        for j in range(1, self.m):
            total = total + self.land[key, j, rows, :].astype(F32)
        return total


def head_peers(h, g):
    me = lax.axis_index("seq")
    slot, part = lax.div(me, g), lax.rem(me, g)
    swaps = [({"seq": lax.rem(slot + d, h) * g + part}) for d in range(1, h)]
    mates = [({"seq": slot * g + lax.rem(part + d, g)}) for d in range(1, g)]
    return slot, part, swaps, mates


def lanes(index, size):
    return pl.ds(pl.multiple_of(index * size, size), size)


class Swap:
    def __init__(self, h, g, send_sem, recv_sem):
        self.h, self.g = h, g
        self.slot, self.part, _, _ = head_peers(h, g)
        self.send_sem, self.recv_sem = send_sem, recv_sem

    def other(self, d):
        return lax.rem(self.slot + d, self.h)

    def device(self, slot):
        return {"seq": slot * self.g + self.part}


def spread_heads(swap, key, source, land, width, offset):
    for d in range(1, swap.h):
        to = swap.other(d)
        remote(
            source.at[pl.ds(pl.multiple_of(to * E, E), E), :],
            land.at[:, lanes(offset + swap.slot, width)],
            swap.send_sem.at[key, d],
            swap.recv_sem.at[key, swap.slot],
            swap.device(to),
        ).start()
    land[:, lanes(offset + swap.slot, width)] = source[
        pl.ds(pl.multiple_of(swap.slot * E, E), E), :
    ]


def spread_wait(swap, key, source, land, width, offset):
    for d in range(1, swap.h):
        src = swap.other(d)
        copy = remote(
            source.at[pl.ds(pl.multiple_of(src * E, E), E), :],
            land.at[:, lanes(offset + src, width)],
            swap.send_sem.at[key, d],
            swap.recv_sem.at[key, src],
            swap.device(src),
        )
        copy.wait_send()
        copy.wait_recv()


def return_copy(swap, key, piece, land, to):
    return remote(
        piece,
        land.at[pl.ds(pl.multiple_of(swap.slot * E, E), E), :],
        swap.send_sem.at[key, to],
        swap.recv_sem.at[key, swap.slot],
        swap.device(to),
    )


def return_wait(swap, key, pieces, land):
    for d in range(1, swap.h):
        src = swap.other(d)
        copy = remote(
            pieces.at[src],
            land.at[pl.ds(pl.multiple_of(src * E, E), E), :],
            swap.send_sem.at[key, src],
            swap.recv_sem.at[key, src],
            swap.device(src),
        )
        copy.wait_send()
        copy.wait_recv()


def mate_copy(part_to, key, d, src, dst, send_sem, recv_sem, slot, part, g):
    return remote(
        src, dst, send_sem.at[key, d], recv_sem.at[key, part], {"seq": slot * g + part_to}
    )


def attn_forward_kernel(
    h,
    g,
    x_ref,
    gain_ref,
    wq_ref,
    wk_ref,
    wv_ref,
    h1_ref,
    qh_ref,
    kv_ref,
    log_ref,
    ah_ref,
    mix_ref,
    local,
    q_land,
    kv_land,
    keys,
    mix_land,
    pieces,
    send_sem,
    recv_sem,
    mate_send,
    mate_recv,
):
    tokens = x_ref.shape[0]
    width = h * tokens
    slot, part, swaps, mates = head_peers(h, g)
    greet(swaps + mates)
    swap = Swap(h, g, send_sem, recv_sem)

    normed, _ = norm_parts(x_ref[...].astype(F32))
    first = (normed * gain_ref[...]).astype(BF16)
    h1_ref[...] = first
    for key, weight in enumerate((wk_ref, wv_ref, wq_ref)):
        local[key] = dot(first, weight[...]).T.astype(BF16)
        if key < 2:
            spread_heads(swap, key, local.at[key], kv_land.at[key], tokens, part * h)
        else:
            spread_heads(swap, key, local.at[key], q_land, tokens, 0)

    for key in range(2):
        spread_wait(swap, key, local.at[key], kv_land.at[key], tokens, part * h)
        mine = kv_land.at[key, :, lanes(part, width)]
        for d in range(1, g):
            mate_copy(
                lax.rem(part + d, g), key, d, mine, mine, mate_send, mate_recv, slot, part, g
            ).start()
    spread_wait(swap, 2, local.at[2], q_land, tokens, 0)
    for key in range(2):
        for d in range(1, g):
            src = lax.rem(part + d, g)
            theirs = kv_land.at[key, :, lanes(src, width)]
            copy = remote(
                theirs,
                theirs,
                mate_send.at[key, d],
                mate_recv.at[key, src],
                {"seq": slot * g + src},
            )
            copy.wait_send()
            copy.wait_recv()

    chunks = g * width // KEY_CHUNK

    @pl.loop(0, chunks)
    def _(c):
        keys[lanes(c, KEY_CHUNK), :] = turn(kv_land[0, :, lanes(c, KEY_CHUNK)])

    @pl.loop(0, h)
    def _(b):
        at = lax.rem(slot + 1 + b, h)
        query = q_land[:, lanes(at, tokens)]

        def step(c, carry):
            peak, total, acc = carry
            scores = dot(keys[lanes(c, KEY_CHUNK), :], query)
            higher = jnp.maximum(peak, jnp.max(scores, axis=0, keepdims=True))
            probs = jnp.exp2((scores - higher) * COEF)
            shrink = jnp.exp2((peak - higher) * COEF)
            total = total * shrink + jnp.sum(probs, axis=0, keepdims=True)
            acc = acc * shrink + dot(kv_land[1, :, lanes(c, KEY_CHUNK)], probs.astype(BF16))
            return higher, total, acc

        start = (
            jnp.full((1, tokens), -jnp.inf, F32),
            jnp.zeros((1, tokens), F32),
            jnp.zeros((E, tokens), F32),
        )
        peak, total, acc = lax.fori_loop(0, chunks, step, start)
        mixed = acc / total
        log_ref[at] = peak * COEF + jnp.log2(total)
        ah_ref[:, lanes(at, tokens)] = mixed
        pieces[at] = mixed.astype(BF16)

        @pl.when(b < h - 1)
        def _():
            return_copy(swap, 3, pieces.at[at], mix_land, at).start()

    mix_land[pl.ds(pl.multiple_of(slot * E, E), E), :] = pieces[slot]
    qh_ref[...] = q_land[...]
    kv_ref[...] = kv_land[...]
    return_wait(swap, 3, pieces, mix_land)
    mix_ref[...] = mix_land[...]


def attn_forward(tokens, gain, wq, wk, wv, n):
    rows, local = tokens.shape[0], wq.shape[1]
    h = local // E
    g = n // h
    width = h * rows
    return vmem_call(
        partial(attn_forward_kernel, h, g),
        [
            ((rows, D), BF16),
            ((E, width), BF16),
            ((2, E, g * width), BF16),
            ((h, 1, rows), F32),
            ((E, width), F32),
            ((local, rows), BF16),
        ],
        [
            pltpu.VMEM((3, local, rows), BF16),
            pltpu.VMEM((E, width), BF16),
            pltpu.VMEM((2, E, g * width), BF16),
            pltpu.VMEM((g * width, E), BF16),
            pltpu.VMEM((local, rows), BF16),
            pltpu.VMEM((h, E, rows), BF16),
            pltpu.SemaphoreType.DMA((4, h)),
            pltpu.SemaphoreType.DMA((4, h)),
            pltpu.SemaphoreType.DMA((2, g)),
            pltpu.SemaphoreType.DMA((2, g)),
        ],
        1,
        "attn_forward",
    )(tokens, gain, wq, wk, wv)


class SeqSum:
    def __init__(self, source, land, total, send_sem, recv_sem, n):
        self.source, self.land, self.total = source, land, total
        self.send_sem, self.recv_sem, self.n = send_sem, recv_sem, n
        self.rows = source.shape[0] // n
        self.fits = source.shape[0] % (8 * n) == 0
        self.me = lax.axis_index("seq")

    def block(self, at):
        return pl.ds(pl.multiple_of(at * self.rows, 8), self.rows)

    def back_copy(self, there, owner):
        part = self.total.at[self.block(owner)]
        return remote(part, part, self.send_sem.at[1], self.recv_sem.at[1], {"seq": there})

    def scatter(self):
        @pl.loop(1, self.n)
        def _(d):
            there = wrap(self.me + d, self.n)
            remote(
                self.source.at[self.block(there)],
                self.land.at[self.me],
                self.send_sem.at[0],
                self.recv_sem.at[0],
                {"seq": there},
            ).start()

        self.land[self.me] = self.source[self.block(self.me), :]

    def gather(self):
        rest = pl.ds(0, self.n - 1)
        copy = remote(
            self.land.at[rest],
            self.land.at[rest],
            self.send_sem.at[0],
            self.recv_sem.at[0],
            {"seq": self.me},
        )
        copy.wait_send()
        copy.wait_recv()
        total = self.land[0]
        for j in range(1, self.n):
            total = total + self.land[j]
        self.total[self.block(self.me), :] = total

        @pl.loop(1, self.n)
        def _(d):
            self.back_copy(wrap(self.me + d, self.n), self.me).start()

    def finish(self):
        part = self.total.at[pl.ds(0, (self.n - 1) * self.rows)]
        copy = remote(part, part, self.send_sem.at[1], self.recv_sem.at[1], {"seq": self.me})
        copy.wait_send()
        copy.wait_recv()


def attn_backward_kernel(
    h,
    g,
    m,
    units,
    ga_ref,
    qh_ref,
    kv_ref,
    log_ref,
    ah_ref,
    h1_ref,
    x_ref,
    gain_ref,
    wq_ref,
    wk_ref,
    wv_ref,
    after_ref,
    base_ref,
    partial_ref,
    text_ref,
    _,
    out_ref,
    final_ref,
    dgain_ref,
    text_out_ref,
    packed_ref,
    done_ref,
    ga_land,
    rows_kv,
    sums,
    pieces,
    halves,
    half_land,
    kv_pieces,
    land,
    cross,
    send_sem,
    recv_sem,
    mate_send,
    mate_recv,
    cross_send,
    cross_recv,
    text_land,
    text_total,
    text_send,
    text_recv,
    dqkv,
    dqkv_sem,
    *ring_scratch,
):
    tokens = x_ref.shape[0]
    width = h * tokens
    n = h * g
    local = ga_ref.shape[0]
    slot, part, swaps, mates = head_peers(h, g)
    me, here = lax.axis_index("seq"), lax.axis_index("mp")
    greet(
        [{"seq": lax.rem(me + d, n)} for d in range(1, n)]
        + [{"mp": lax.rem(here + d, m)} for d in range(1, m)]
    )
    swap = Swap(h, g, send_sem, recv_sem)
    mp_sum = Exchange(cross, cross_send, cross_recv, m)

    spread_heads(swap, 0, ga_ref, ga_land, tokens, 0)
    everything = pl.ds(0, tokens)
    mp_sum.send(1, everything, partial_ref[...])
    piece = done_ref.shape[0] // (RINGS * n)
    ring = RingSum(n, piece, True, packed_ref, done_ref, ring_scratch)
    ring.start()
    text_sum = SeqSum(text_ref, text_land, text_total, text_send, text_recv, n)
    if text_sum.fits:
        text_sum.scatter()
    chunks = g * width // KEY_CHUNK

    @pl.loop(0, chunks)
    def _(c):
        for key in range(2):
            rows_kv[key, lanes(c, KEY_CHUNK), :] = turn(kv_ref[key, :, lanes(c, KEY_CHUNK)])
            sums[key, lanes(c, KEY_CHUNK), :] = jnp.zeros((KEY_CHUNK, E), F32)

    spread_wait(swap, 0, ga_ref, ga_land, tokens, 0)
    ring.first()
    in_loop = chunks % 2 == 0 and 2 * h <= ring.ticks_all
    ring.next = 2 * h if in_loop else 0

    def one_block(b):
        at = lax.rem(slot + 1 + b, h)
        query = qh_ref[:, lanes(at, tokens)]
        grad = ga_land[:, lanes(at, tokens)]
        query_rows, grad_rows = turn(query), turn(grad)
        level = log_ref[at]
        inner = jnp.sum(grad.astype(F32) * ah_ref[:, lanes(at, tokens)], axis=0, keepdims=True)

        def step(c, acc):
            here_rows = lanes(c, KEY_CHUNK)
            scores = dot(rows_kv[0, here_rows, :], query)
            probs = jnp.exp2(scores * COEF - level)
            grad_probs = dot(rows_kv[1, here_rows, :], grad)
            grad_scores = (probs * (grad_probs - inner)).astype(BF16)
            sums[0, here_rows, :] += dot(grad_scores, query_rows)
            sums[1, here_rows, :] += dot(probs.astype(BF16), grad_rows)
            return acc + dot(kv_ref[0, :, here_rows], grad_scores)

        acc = jnp.zeros((E, tokens), F32)
        for k in range(2):
            acc = lax.fori_loop(k * chunks // 2, (k + 1) * chunks // 2, step, acc)
            if in_loop:
                ring.tick(2 * b + k)
        pieces[at] = (acc * SCALE).astype(BF16)

        @pl.when(b < h - 1)
        def _():
            return_copy(swap, 1, pieces.at[at], land.at[0], at).start()

    pl.loop(0, h)(one_block)

    for key, factor in ((0, SCALE), (1, 1.0)):
        for d in range(1, g):
            to = lax.rem(part + d, g)

            @pl.loop(0, h)
            def _(i):
                block = sums[key, lanes(to * h + i, tokens), :] * factor
                halves[key, d, :, lanes(i, tokens)] = block.T.astype(BF16)

            remote(
                halves.at[key, d],
                half_land.at[key, part],
                mate_send.at[key, d],
                mate_recv.at[key, part],
                {"seq": slot * g + to},
            ).start()
    if text_sum.fits:
        text_sum.gather()
    ring.idle(3)
    for key, factor in ((0, SCALE), (1, 1.0)):
        for d in range(1, g):
            src = lax.rem(part + d, g)
            copy = remote(
                halves.at[key, d],
                half_land.at[key, src],
                mate_send.at[key, d],
                mate_recv.at[key, src],
                {"seq": slot * g + src},
            )
            copy.wait_send()
            copy.wait_recv()

        @pl.loop(0, h)
        def _(b):
            at = lax.rem(slot + 1 + b, h)
            total = (sums[key, lanes(part * h + at, tokens), :] * factor).T
            for d in range(1, g):
                src = lax.rem(part + d, g)
                total = total + half_land[key, src, :, lanes(at, tokens)].astype(F32)
            kv_pieces[key, at] = total.astype(BF16)

            @pl.when(b < h - 1)
            def _():
                return_copy(swap, 2 + key, kv_pieces.at[key, at], land.at[1 + key], at).start()

    mine = pl.ds(pl.multiple_of(slot * E, E), E)
    land[0, mine, :] = pieces[slot]
    land[1, mine, :] = kv_pieces[0, slot]
    land[2, mine, :] = kv_pieces[1, slot]
    ring.idle(3)
    return_wait(swap, 1, pieces, land.at[0])
    return_wait(swap, 2, kv_pieces.at[0], land.at[1])
    return_wait(swap, 3, kv_pieces.at[1], land.at[2])

    grads = [turn(land[key]) for key in range(3)]
    partial_sum = dot_nt(grads[0], wq_ref[...])
    partial_sum = partial_sum + dot_nt(grads[1], wk_ref[...])
    partial_sum = partial_sum + dot_nt(grads[2], wv_ref[...])
    mp_sum.send(0, everything, partial_sum)
    first = turn(h1_ref[...])
    for key in range(3):
        product = dot(first, grads[key]).astype(BF16)
        for k in range(local // 128):
            row = (key * (local // 128) + k) * D
            dqkv[row : row + D, :] = product[:, k * 128 : (k + 1) * 128]
    start = packed_sections(local, 0)[3][0] + 2 * D // 128 * units
    store = pltpu.make_async_copy(
        dqkv, packed_ref.at[pl.ds(start, dqkv.shape[0])], dqkv_sem.at[0]
    )
    store.start()
    if text_sum.fits:
        text_sum.finish()
        text_out_ref[...] = text_total[...].astype(BF16)
    else:
        text_out_ref[...] = text_ref[...].astype(BF16)
    ring.idle(4)
    final_ref[...] = (base_ref[...] + mp_sum.wait(1, everything)).astype(BF16)
    normed, inverse = norm_parts(x_ref[...].astype(F32))
    total = mp_sum.wait(0, everything)
    into, gain_grad = norm_back(total, normed, inverse, gain_ref[...])
    out_ref[...] = after_ref[...] + into
    dgain_ref[...] = gain_grad
    store.wait()
    ring.finish()


def attn_backward(ga, qh, kv, log, ah, h1, tokens, gain, wq, wk, wv, after, base, partial_out, text, packed, units, n, m):
    rows, local = tokens.shape[0], wq.shape[1]
    h = local // E
    g = n // h
    width = h * rows
    split, total = packed_split(local, units, n)
    return vmem_call(
        partial(attn_backward_kernel, h, g, m, units),
        [
            ((rows, D), F32),
            ((rows, D), BF16),
            ((1, D), F32),
            (text.shape, BF16),
            (packed.shape, BF16),
            ((split, 128), BF16),
        ],
        [
            pltpu.VMEM((E, width), BF16),
            pltpu.VMEM((2, g * width, E), BF16),
            pltpu.VMEM((2, g * width, E), F32),
            pltpu.VMEM((h, E, rows), BF16),
            pltpu.VMEM((2, g, E, width), BF16),
            pltpu.VMEM((2, g, E, width), BF16),
            pltpu.VMEM((2, h, E, rows), BF16),
            pltpu.VMEM((3, local, rows), BF16),
            pltpu.VMEM((2, m, rows, D), BF16),
            pltpu.SemaphoreType.DMA((4, h)),
            pltpu.SemaphoreType.DMA((4, h)),
            pltpu.SemaphoreType.DMA((2, g)),
            pltpu.SemaphoreType.DMA((2, g)),
            pltpu.SemaphoreType.DMA((2, m)),
            pltpu.SemaphoreType.DMA((2, m)),
            pltpu.VMEM((n, max(text.shape[0] // n, 8), text.shape[1]), F32),
            pltpu.VMEM(text.shape, F32),
            pltpu.SemaphoreType.DMA((2,)),
            pltpu.SemaphoreType.DMA((2,)),
            pltpu.VMEM((3 * local // 128 * D, 128), BF16),
            pltpu.SemaphoreType.DMA((1,)),
        ]
        + RingSum.scratch(n, split // (RINGS * n), True),
        2,
        "attn_backward",
        in_any=(15,),
        out_any=(4, 5),
        aliases={15: 4},
    )(ga, qh, kv, log, ah, h1, tokens, gain, wq, wk, wv, after, base, partial_out, text, packed)


def middle_kernel(
    m,
    mix_ref,
    x_ref,
    og_ref,
    wo_ref,
    gain2_ref,
    cq_ref,
    k2_ref,
    v2_ref,
    co_ref,
    gain3_ref,
    wu_ref,
    bu_ref,
    wd_ref,
    bd_ref,
    base_ref,
    units_sum_ref,
    after_ref,
    ga_ref,
    text_ref,
    packed_ref,
    dgain2_ref,
    dgain3_ref,
    dup_ref,
    ddown_ref,
    h2_ref,
    gq2_ref,
    a2_ref,
    go2_ref,
    go_ref,
    h3_ref,
    gz_ref,
    u_ref,
    packed,
    packed_sem,
    back_units,
    x1,
    x2,
    q2,
    probs,
    kd,
    kdt,
    vd,
    vdt,
    land,
    send_sem,
    recv_sem,
):
    here = lax.axis_index("mp")
    greet([{"mp": lax.rem(here + d, m)} for d in range(1, m)])
    mp_sum = Exchange(land, send_sem, recv_sem, m)
    total_rows = x_ref.shape[0]
    rows = total_rows // 2
    blocks = [pl.ds(b * rows, rows) for b in range(2)]
    full = pl.ds(0, rows)
    text, local = k2_ref.shape
    units = wu_ref.shape[1]
    pairs = local // 128
    chunk = min(512, units)

    mixed = turn(mix_ref[...])
    for b in range(2):
        mp_sum.send(b, full, dot(mixed[b * rows : (b + 1) * rows], wo_ref[...]))

    low_lane = lax.broadcasted_iota(jnp.int32, (text, 128), 1) < E
    for p in range(pairs):
        cols = slice(p * 128, (p + 1) * 128)
        for source, plain, turned in ((k2_ref, kd, kdt), (v2_ref, vd, vdt)):
            both = source[:, cols].astype(F32)
            stacked = jnp.concatenate(
                [jnp.where(low_lane, both, 0.0), jnp.where(low_lane, 0.0, both)], axis=0
            )
            plain[p] = stacked.astype(BF16)
            turned[p] = stacked.T.astype(BF16)

    ddown_ref[...] = jnp.sum(og_ref[...].astype(F32), axis=0, keepdims=True)
    for b in range(2):

        @pl.loop(0, units // chunk)
        def _(c):
            cols = lanes(c, chunk)
            back_units[blocks[b], cols] = dot_nt(og_ref[blocks[b], :], wd_ref[cols, :])

    for b in range(2):
        at = blocks[b]
        x1[at, :] = x_ref[at, :].astype(F32) + mp_sum.wait(b, full)
        normed, _ = norm_parts(x1[at, :])
        second = (normed * gain2_ref[...]).astype(BF16)
        h2_ref[at, :] = second
        q2[at, :] = dot(second, cq_ref[...]).astype(BF16)
        for p in range(pairs):
            cols = slice(p * 128, (p + 1) * 128)
            scores = dot(q2[at, cols], kdt[p]) * SCALE
            parts = []
            for i in range(2):
                one = scores[:, i * text : (i + 1) * text]
                expo = jnp.exp(one - jnp.max(one, axis=-1, keepdims=True))
                parts.append(expo / jnp.sum(expo, axis=-1, keepdims=True))
            prob = jnp.concatenate(parts, axis=1)
            probs[p, at, :] = prob
            a2_ref[at, cols] = dot(prob.astype(BF16), vd[p]).astype(BF16)
        mp_sum.send(2 + b, full, dot(a2_ref[at, :], co_ref[...]))

    for b in range(2):
        at = blocks[b]
        x2[at, :] = x1[at, :] + mp_sum.wait(2 + b, full)
        normed, _ = norm_parts(x2[at, :])
        h3_ref[at, :] = (normed * gain3_ref[...]).astype(BF16)

        @pl.loop(0, units // chunk)
        def _(c):
            cols = lanes(c, chunk)
            z = dot(h3_ref[at, :], wu_ref[:, cols]) + bu_ref[:, cols]
            cdf = 0.5 + 0.5 * lax.erf(z * math.sqrt(0.5))
            slope = cdf + z * (jnp.exp(z * z * -0.5) * (1.0 / math.sqrt(2.0 * math.pi)))
            u_ref[at, cols] = (z * cdf).astype(BF16)
            gz = (back_units[at, cols] * slope).astype(BF16)
            gz_ref[at, cols] = gz
            bias = jnp.sum(gz.astype(F32), axis=0, keepdims=True)
            if b == 0:
                dup_ref[:, cols] = bias
            else:
                dup_ref[:, cols] += bias

        mp_sum.send(4 + b, full, dot_nt(gz_ref[at, :], wu_ref[...]))

    for b in range(2):
        at = blocks[b]
        units_sum_ref[at, :] = dot(u_ref[at, :], wd_ref[...]).astype(BF16)
        base_ref[at, :] = x2[at, :] + bd_ref[...]

    sections = packed_sections(local, units)[:5]

    def section_copy(which):
        start, count = sections[which][0], sections[which][1] * sections[which][2]
        rows_here = pl.ds(start, count)
        return pltpu.make_async_copy(
            packed.at[rows_here], packed_ref.at[rows_here], packed_sem.at[which]
        )

    def weight_grad(which, left, right_ref):
        start, count, height = sections[which]
        step = 4 if count % 4 == 0 else 1

        @pl.loop(0, count // step)
        def _(c):
            product = dot(left, right_ref[:, lanes(c, step * 128)]).astype(BF16)
            for k in range(step):
                place = pl.multiple_of(start + (c * step + k) * height, 16)
                packed[pl.ds(place, height), :] = product[:, k * 128 : (k + 1) * 128]

        section_copy(which).start()

    weight_grad(3, turn(h3_ref[...]), gz_ref)
    weight_grad(4, turn(u_ref[...]), og_ref)

    for b in range(2):
        at = blocks[b]
        normed, inverse = norm_parts(x2[at, :])
        into, gain_grad = norm_back(mp_sum.wait(4 + b, full), normed, inverse, gain3_ref[...])
        after = og_ref[at, :].astype(F32) + into
        x2[at, :] = after
        go2 = after.astype(BF16)
        go2_ref[at, :] = go2
        ga2 = dot_nt(go2, co_ref[...]).astype(BF16)
        for p in range(pairs):
            cols = slice(p * 128, (p + 1) * 128)
            prob = probs[p, at, :]
            grad_prob = dot(ga2[:, cols], vdt[p])
            parts = []
            for i in range(2):
                half = slice(i * text, (i + 1) * text)
                one, grad_one = prob[:, half], grad_prob[:, half]
                inner = jnp.sum(one * grad_one, axis=-1, keepdims=True)
                parts.append(one * (grad_one - inner))
            grad_scores = jnp.concatenate(parts, axis=1)
            gq2_ref[at, cols] = (dot(grad_scores.astype(BF16), kd[p]) * SCALE).astype(BF16)
            both = dot(grad_scores.T.astype(BF16), q2[at, cols]) * SCALE
            key_part = jnp.where(low_lane, both[:text], both[text:])
            both = dot(prob.T.astype(BF16), ga2[:, cols])
            value_part = jnp.where(low_lane, both[:text], both[text:])
            late = slice(local + p * 128, local + (p + 1) * 128)
            if b == 0:
                text_ref[:, cols] = key_part
                text_ref[:, late] = value_part
            else:
                text_ref[:, cols] += key_part
                text_ref[:, late] += value_part
        mp_sum.send(6 + b, full, dot_nt(gq2_ref[at, :], cq_ref[...]))
        if b == 0:
            dgain3_ref[...] = gain_grad
        else:
            dgain3_ref[...] += gain_grad

    weight_grad(0, turn(h2_ref[...]), gq2_ref)
    weight_grad(1, turn(a2_ref[...]), go2_ref)
    for b in range(2):
        at = blocks[b]
        normed, inverse = norm_parts(x1[at, :])
        into, gain_grad = norm_back(mp_sum.wait(6 + b, full), normed, inverse, gain2_ref[...])
        after = x2[at, :] + into
        after_ref[at, :] = after
        go = after.astype(BF16)
        go_ref[at, :] = go
        ga_ref[:, b * rows : (b + 1) * rows] = dot_nt(go, wo_ref[...]).T.astype(BF16)
        if b == 0:
            dgain2_ref[...] = gain_grad
        else:
            dgain2_ref[...] += gain_grad
    weight_grad(2, mix_ref[...], go_ref)
    extra = slice(2 * local, 2 * local + 128)
    text_ref[:, extra] = jnp.zeros((text, 128), F32)
    row = 0
    for vector in (dgain2_ref, dgain3_ref, dup_ref, ddown_ref):
        for i in range(vector.shape[1] // 128):
            text_ref[row : row + 1, extra] = vector[:, i * 128 : (i + 1) * 128]
            row += 1
    for which in range(len(sections)):
        section_copy(which).wait()


def packed_sections(local, units):
    sections, start = [], 0
    for count, height in (
        (local // 128, D),
        (D // 128, local),
        (D // 128, local),
        (units // 128, D),
        (D // 128, units),
        (local // 128, D),
        (local // 128, D),
        (local // 128, D),
    ):
        sections.append((start, count, height))
        start += count * height
    return sections


def packed_split(local, units, n):
    start, count, height = packed_sections(local, units)[-1]
    grain = RINGS * n * 16
    total = -(-(start + count * height) // grain) * grain
    start, count, height = packed_sections(local, units)[2]
    return max((start + count * height) // grain, 1) * grain, total


def unpack(first, second, local, units):
    split = first.shape[0]
    parts = []
    for start, count, height in packed_sections(local, units):
        if start + count * height <= split:
            part = first[start : start + count * height]
        elif start >= split:
            part = second[start - split : start - split + count * height]
        else:
            part = jnp.concatenate([first[start:], second[: start - split + count * height]])
        part = part.reshape(count, height, 128)
        parts.append(part.transpose(1, 0, 2).reshape(height, count * 128).astype(F32))
    return parts


def middle(mix, tokens, og, wo, gain2, cq, k2, v2, co, gain3, wu, bu, wd, bd, n, m):
    rows, (text, local), units = tokens.shape[0], k2.shape, wu.shape[1]
    pairs = local // 128
    _, total = packed_split(local, units, n)
    mine = packed_sections(local, units)[5][0]
    return vmem_call(
        partial(middle_kernel, m),
        [
            ((rows, D), F32),
            ((rows, D), BF16),
            ((rows, D), F32),
            ((local, rows), BF16),
            ((text, 2 * local + 128), F32),
            ((total, 128), BF16),
        ],
        [
            pltpu.VMEM((1, D), F32),
            pltpu.VMEM((1, D), F32),
            pltpu.VMEM((1, units), F32),
            pltpu.VMEM((1, D), F32),
            pltpu.VMEM((rows, D), BF16),
            pltpu.VMEM((rows, local), BF16),
            pltpu.VMEM((rows, local), BF16),
            pltpu.VMEM((rows, D), BF16),
            pltpu.VMEM((rows, D), BF16),
            pltpu.VMEM((rows, D), BF16),
            pltpu.VMEM((rows, units), BF16),
            pltpu.VMEM((rows, units), BF16),
            pltpu.VMEM((mine, 128), BF16),
            pltpu.SemaphoreType.DMA((5,)),
            pltpu.VMEM((rows, units), F32),
            pltpu.VMEM((rows, D), F32),
            pltpu.VMEM((rows, D), F32),
            pltpu.VMEM((rows, local), BF16),
            pltpu.VMEM((pairs, rows, 2 * text), F32),
            pltpu.VMEM((pairs, 2 * text, 128), BF16),
            pltpu.VMEM((pairs, 128, 2 * text), BF16),
            pltpu.VMEM((pairs, 2 * text, 128), BF16),
            pltpu.VMEM((pairs, 128, 2 * text), BF16),
            pltpu.VMEM((8, m, rows // 2, D), BF16),
            pltpu.SemaphoreType.DMA((8, m)),
            pltpu.SemaphoreType.DMA((8, m)),
        ],
        3,
        "middle",
        out_any=(5,),
    )(mix, tokens, og, wo, gain2, cq, k2, v2, co, gain3, wu, bu, wd, bd)


def ring_chip(place, chips):
    if chips % 2:
        return place
    half = chips // 2
    return jnp.where(place < half, 2 * place, 2 * (chips - 1 - place) + 1)


def ring_place(chip, chips):
    if chips % 2:
        return chip
    z, x = lax.div(chip, 2), lax.rem(chip, 2)
    return jnp.where(x == 0, z, chips - 1 - z)


class RingSum:
    SCRATCH = (
        "pair",
        "land",
        "stage",
        "send_sem",
        "recv_sem",
        "pair_send",
        "pair_recv",
        "out_send",
        "out_recv",
        "stage_sem",
        "keep_sem",
    )

    @staticmethod
    def scratch(n, piece, staged):
        dma, chips = pltpu.SemaphoreType.DMA, n // 2
        return [
            pltpu.VMEM((RINGS, chips, piece, 128), BF16),
            pltpu.VMEM((RINGS, chips - 1, piece, 128), BF16),
            pltpu.VMEM((RINGS, 2, piece, 128) if staged else (1, 1, 16, 128), BF16),
            dma((RINGS, 2 * chips)),
            dma((RINGS, 2 * chips)),
            dma((RINGS, chips)),
            dma((RINGS, chips)),
            dma((RINGS, chips)),
            dma((RINGS, chips)),
            dma((RINGS, 2)),
            dma((RINGS,)),
        ]

    def __init__(self, n, piece, staged, own, done, scratch, base=0):
        self.__dict__.update(zip(self.SCRATCH, scratch))
        self.own, self.done, self.base = own, done, base
        self.piece, self.staged = piece, staged
        self.chips, self.steps = n // 2, n // 2 - 1
        me = lax.axis_index("seq")
        chip, self.core = lax.div(me, 2), lax.rem(me, 2)
        place = ring_place(chip, self.chips)
        self.mate = {"seq": 2 * chip + 1 - self.core}
        after = 2 * ring_chip(wrap(place + 1, self.chips), self.chips) + self.core
        before = 2 * ring_chip(wrap(place - 1, self.chips), self.chips) + self.core
        self.ways = [
            (place, {"seq": after}),
            (wrap(self.chips - place, self.chips), {"seq": before}),
        ]
        self.half = RINGS * self.chips * piece
        self.groups = RINGS // 2
        self.next = 0
        self.ticks_all = self.groups * (2 * self.steps - 1)

    def chunk(self, v, t):
        return wrap(v - t, self.chips)

    def rows(self, core, q, chunk, base=0):
        start = base + core * self.half + (q * self.chips + chunk) * self.piece
        return pl.ds(pl.multiple_of(start, 16), self.piece)

    def ring_copy(self, src, dst, q, t, to):
        return remote(src, dst, self.send_sem.at[q, t], self.recv_sem.at[q, t], to)

    def pair_copy(self, q, v, t):
        chunk = self.chunk(v, t)
        return remote(
            self.own.at[self.rows(1 - self.core, q, chunk, self.base)],
            self.pair.at[q, chunk],
            self.pair_send.at[q, t],
            self.pair_recv.at[q, t],
            self.mate,
        )

    def out_copy(self, src, there, q, k):
        return remote(src, there, self.out_send.at[q, k], self.out_recv.at[q, k], self.mate)

    def fetch(self, q, v, t, slot):
        return pltpu.make_async_copy(
            self.own.at[self.rows(self.core, q, self.chunk(v, t), self.base)],
            self.stage.at[q, slot],
            self.stage_sem.at[q, slot],
        )

    def keep(self, q, v):
        return pltpu.make_async_copy(
            self.land.at[q, self.steps - 1],
            self.done.at[self.rows(self.core, q, wrap(v + 1, self.chips))],
            self.keep_sem.at[q],
        )

    def mine(self, q, v, t, slot):
        chunk = self.chunk(v, t)
        if self.staged:
            self.fetch(q, v, t, slot).wait()
            part = self.stage[q, slot]
        else:
            part = self.own[self.rows(self.core, q, chunk, self.base), :]
        self.pair_copy(q, v, t).wait_recv()
        return part.astype(F32) + self.pair[q, chunk].astype(F32)

    def start(self):
        for t in range(2):
            for q in range(RINGS):
                v, _ = self.ways[q % 2]
                self.pair_copy(q, v, t).start()
                if self.staged:
                    self.fetch(q, v, t, t).start()

    def first(self):
        for q in range(RINGS):
            v, to = self.ways[q % 2]
            here = self.pair.at[q, v]
            self.pair[q, v] = self.mine(q, v, 0, 0).astype(BF16)
            self.ring_copy(here, self.land.at[q, 0], q, 0, to).start()

    def tick(self, u):
        steps = self.steps
        t = lax.div(u, self.groups) + 1
        group = lax.rem(u, self.groups)
        slot = lax.rem(t, 2)

        @pl.when(t <= steps)
        def _():
            for way in range(2):
                v, to = self.ways[way]
                q = 2 * group + way

                @pl.when(t < steps)
                def _():
                    self.pair_copy(q, v, t + 1).start()
                    if self.staged:
                        self.fetch(q, v, t + 1, 1 - slot).start()

                here = self.land.at[q, t - 1]
                mine = self.mine(q, v, t, slot)
                self.ring_copy(here, here, q, t - 1, to).wait_recv()
                self.land[q, t - 1] = (self.land[q, t - 1].astype(F32) + mine).astype(BF16)

                @pl.when(t < steps)
                def _():
                    self.ring_copy(here, self.land.at[q, t], q, t, to).start()

                @pl.when(t == steps)
                def _():
                    there = self.done.at[self.rows(self.core, q, wrap(v + 1, self.chips))]
                    self.ring_copy(here, there, q, t, to).start()
                    self.out_copy(here, there, q, 0).start()
                    self.keep(q, v).start()

        @pl.when(t > steps)
        def _():
            for way in range(2):
                v, to = self.ways[way]
                q = 2 * group + way
                k = t - steps
                part = self.done.at[self.rows(self.core, q, self.chunk(v + 1, k))]
                self.ring_copy(part, part, q, t - 1, to).wait_recv()
                self.ring_copy(part, part, q, t, to).start()
                self.out_copy(part, part, q, k).start()

    def loop(self, count, ticks, body):
        ticks = max(min(ticks, self.ticks_all - self.next, count), 0)
        if ticks == 0:
            pl.loop(0, count)(body)
            return
        first = self.next
        self.next += ticks
        every = count // ticks

        @pl.loop(0, ticks)
        def _(k):
            @pl.loop(0, every)
            def _(i):
                body(k * every + i)

            self.tick(first + k)

        if ticks * every < count:
            pl.loop(ticks * every, count)(body)

    def idle(self, count):
        count = min(count, self.ticks_all - self.next)
        first = self.next
        self.next += count
        if count:
            pl.loop(first, first + count)(self.tick)

    def finish(self):
        self.idle(self.ticks_all)
        last = 2 * self.steps
        for q in range(RINGS):
            v, to = self.ways[q % 2]
            part = self.done.at[self.rows(self.core, q, self.chunk(v + 1, self.steps))]
            self.ring_copy(part, part, q, last - 1, to).wait_recv()
            self.out_copy(part, part, q, self.steps).start()
            self.keep(q, v).wait()

        @pl.loop(0, last)
        def _(t):
            for q in range(RINGS):
                v, to = self.ways[q % 2]
                self.ring_copy(self.land.at[q, 0], self.land.at[q, 0], q, t, to).wait_send()

        @pl.loop(0, self.chips)
        def _(t):
            for q in range(RINGS):
                v, _ = self.ways[q % 2]
                self.pair_copy(q, v, t).wait_send()
                other = self.done.at[self.rows(1 - self.core, q, self.chunk(v + 1, t))]
                copy = self.out_copy(other, other, q, t)
                copy.wait_send()
                copy.wait_recv()


GROUP = 8


def fold(values):
    total = values[:, :128]
    for i in range(1, values.shape[1] // 128):
        total = total + values[:, i * 128 : (i + 1) * 128]
    return total


def wide(columns, width):
    return jnp.concatenate([columns] * (width // 128), axis=1) if width > 128 else columns


def silu_parts(scaled):
    gate = jax.nn.sigmoid(scaled)
    return scaled * gate, gate * (1.0 + scaled * (1.0 - gate))


def pack_sums(columns):
    lane = lax.broadcasted_iota(jnp.int32, (8, 128), 1)
    tile = jnp.zeros((8, 128), F32)
    for q, sums in enumerate(columns):
        groups = sums.shape[0] // GROUP
        line = jnp.sum(sums, axis=1, keepdims=True)
        for t in range(groups):
            tile = jnp.where(lane == q * groups + t, line[t * GROUP : (t + 1) * GROUP], tile)
    return tile


def unpack_sums(tile, count, channels):
    groups = channels // GROUP
    row = jnp.sum(tile, axis=0, keepdims=True)
    turned = jnp.broadcast_to(row, (128, 128)).T
    blocks = []
    for q in range(count):
        part = turned[q * groups : (q + 1) * groups]
        part = jnp.broadcast_to(part[:, None, :], (groups, GROUP, 128))
        blocks.append(part.reshape(channels, 128))
    return blocks


def put_shifted(stack, row, values):
    width = values.shape[1]
    lane = lax.broadcasted_iota(jnp.int32, values.shape, 1)
    stack[row, 0] = jnp.where(lane == 0, 0.0, pltpu.roll(values, 1, 1)).astype(BF16)
    stack[row, 1] = values.astype(BF16)
    stack[row, 2] = jnp.where(lane == width - 1, 0.0, pltpu.roll(values, width - 1, 1)).astype(BF16)


def three_rows(stack, row):
    return stack[pl.ds(row, 3)].reshape(9 * stack.shape[2], stack.shape[3])


class ConvMap:
    INPUTS = ("gain_one", "gain_two", "shift", "weight_one", "weight_two")
    OUTPUTS = ("out", "grad")
    SCRATCH = (
        "feats",
        "cot",
        "act",
        "stack_two",
        "wt1",
        "wt2",
        "wb2",
        "wb1",
        "raw",
        "hid",
        "send_both",
        "got_two",
        "got_one",
        "gains",
        "norm_one",
        "norm_two",
        "acc",
        "vec",
    )

    def __init__(self, index, n, m, sources, refs, sems):
        self.index, self.n, self.m = index, n, m
        self.sources = sources
        self.__dict__.update(refs)
        self.__dict__.update(sems)
        self.rows, self.local, self.width = self.out.shape
        self.chans = self.feats.shape[1]
        self.me, self.here = lax.axis_index("seq"), lax.axis_index("mp")
        self.high = self.rows * n
        self.count = float(self.high * self.width * GROUP)
        self.own = pl.ds(pl.multiple_of(self.here * self.local, self.local), self.local)
        self.step = max(self.rows // 4, 2)

    def ticks(self, crop, mid):
        return (crop, mid)[self.index]

    def peer(self, d):
        return lax.rem(self.here + d, self.m)

    def loads(self, which):
        full = (self.feats, self.cot)[which]
        copies = []
        for d in range(self.m):
            chans = pl.ds(pl.multiple_of(self.peer(d) * self.local, self.local), self.local)
            copies.append(
                pltpu.make_async_copy(
                    self.sources[which][d],
                    full.at[pl.ds(2, self.rows), chans, :],
                    self.load_sem.at[self.index, which, d],
                )
            )
        return copies

    def gain_copies(self):
        return [
            remote(
                self.gain_one,
                self.gains.at[self.own, :],
                self.gain_send.at[self.index, d],
                self.gain_recv.at[self.index, d],
                {"mp": self.peer(d)},
            )
            for d in range(1, self.m)
        ]

    def edges(self, which):
        full, rows = (self.feats, self.cot)[which], self.rows
        up = remote(
            full.at[pl.ds(2, 2)],
            full.at[pl.ds(rows + 2, 2)],
            self.edge_send.at[self.index, which, 0],
            self.edge_recv.at[self.index, which, 0],
            {"seq": jnp.maximum(self.me - 1, 0)},
        )
        down = remote(
            full.at[pl.ds(rows, 2)],
            full.at[pl.ds(0, 2)],
            self.edge_send.at[self.index, which, 1],
            self.edge_recv.at[self.index, which, 1],
            {"seq": jnp.minimum(self.me + 1, self.n - 1)},
        )
        return up, down

    def start_edges(self, which):
        up, down = self.edges(which)
        full, rows = (self.feats, self.cot)[which], self.rows
        blank = jnp.zeros((2,) + full.shape[1:], BF16)

        @pl.when(self.me > 0)
        def _():
            up.start()

        @pl.when(self.me == 0)
        def _():
            full[pl.ds(0, 2)] = blank

        @pl.when(self.me < self.n - 1)
        def _():
            down.start()

        @pl.when(self.me == self.n - 1)
        def _():
            full[pl.ds(rows + 2, 2)] = blank

    def wait_edges(self, which):
        up, down = self.edges(which)

        @pl.when(self.me > 0)
        def _():
            up.wait_send()
            down.wait_recv()

        @pl.when(self.me < self.n - 1)
        def _():
            down.wait_send()
            up.wait_recv()

    def stat_copy(self, key, part, there):
        return remote(
            part, part, self.stat_send.at[key], self.stat_recv.at[key], {"seq": there}
        )

    def send_stats(self, e, tile):
        key = 4 * self.index + e
        self.stat[key, self.me] = tile

        @pl.loop(1, self.n)
        def _(d):
            part = self.stat.at[key, self.me]
            self.stat_copy(key, part, wrap(self.me + d, self.n)).start()

    def sum_stats(self, e):
        key = 4 * self.index + e
        copy = self.stat_copy(key, self.stat.at[key, pl.ds(0, self.n - 1)], self.me)
        copy.wait_send()
        copy.wait_recv()
        total = self.stat[key, 0]
        for j in range(1, self.n):
            total = total + self.stat[key, j]
        return total

    def wait_stats(self, e, channels):
        return unpack_sums(self.sum_stats(e), 2, channels)

    def clear(self, count):
        for q in range(count):
            self.acc[q] = jnp.zeros(self.acc.shape[1:], F32)

    def valid(self, row):
        at = self.me * self.rows + row
        return jnp.logical_and(at >= 0, at < self.high)

    def inside(self, e):
        return jnp.logical_and(e >= 1, e <= self.rows).astype(F32)

    def wide(self, columns):
        return wide(columns, self.width)

    def lay_out_weights(self):
        chans, local = self.chans, self.local
        for i in range(3):
            for j in range(3):
                tap = 3 * i + j
                one, two = self.weight_one[i, j], self.weight_two[i, j]
                rows = slice(j * local, (j + 1) * local)
                self.wt1[rows, i * chans : (i + 1) * chans] = turn(one)
                self.wt2[:, tap * local : (tap + 1) * local] = turn(two)
                rows = slice((2 - j) * local, (3 - j) * local)
                self.wb2[rows, (2 - i) * chans : (3 - i) * chans] = two
                self.wb1[:, (8 - tap) * local : (9 - tap) * local] = one

    def row_pairs(self):
        return 256 // self.width if self.width < 256 and self.rows % 2 == 0 else 1

    def conv_all(self, weights, source, ticks, use):
        together, local, width = self.row_pairs(), self.local, self.width
        taps_in = 3 * self.chans

        def body(step):
            first = step * together
            side = [source[pl.ds(first + k, 3)].reshape(taps_in, width) for k in range(together)]
            block = jnp.concatenate(side, axis=1) if together > 1 else side[0]
            products = dot(weights[...], block)
            lane = lax.broadcasted_iota(jnp.int32, (local, width), 1)
            for k in range(together):
                cols = slice(k * width, (k + 1) * width)
                left, middle, right = [
                    products[j * local : (j + 1) * local, cols] for j in range(3)
                ]
                left = jnp.where(lane == 0, 0.0, pltpu.roll(left, 1, 1))
                right = jnp.where(lane == width - 1, 0.0, pltpu.roll(right, width - 1, 1))
                use(first + k, left + middle + right)

        self.back.loop((self.rows + 2) // together, ticks, body)

    def first_sums(self):
        self.clear(2)

        @pl.loop(0, self.rows)
        def _(y):
            values = self.feats[y + 2].astype(F32)
            self.acc[0] += fold(values)
            self.acc[1] += fold(values * values)

        self.send_stats(0, pack_sums([self.acc[0], self.acc[1]]))

    def back_two(self):
        def use(e, values):
            self.raw[e] = values

        self.conv_all(self.wb2, self.cot, self.ticks(4, 1), use)

    def norm_of(self, total, squares):
        mean = total / self.count
        return mean, lax.rsqrt(squares / self.count - mean * mean + 1e-05)

    def conv_one(self):
        mean, inverse = self.norm_of(*self.wait_stats(0, self.chans))
        self.norm_one[0], self.norm_one[1] = mean, inverse
        gains = self.gains[...]
        scale = inverse * gains
        offset = -mean * scale
        self.norm_one[2], self.norm_one[3] = scale, offset

        def activate(r):
            scaled = self.feats[r].astype(F32) * self.wide(self.norm_one[2])
            scaled = scaled + self.wide(self.norm_one[3])
            act = scaled * jax.nn.sigmoid(scaled)
            self.act[r] = jnp.where(self.valid(r - 2), act, 0.0).astype(BF16)

        self.back.loop(self.rows + 4, self.ticks(1, 1), activate)
        self.clear(2)

        def use(e, values):
            hid = values + self.wide(self.shift[...])
            self.hid[e] = hid
            mine = self.inside(e)
            self.acc[0, : self.local] += fold(hid) * mine
            self.acc[1, : self.local] += fold(hid * hid) * mine

        self.conv_all(self.wt1, self.act, self.ticks(4, 1), use)
        self.send_stats(1, pack_sums([self.acc[0, : self.local], self.acc[1, : self.local]]))

    def second_norm(self, e):
        normed = (self.hid[e] - self.wide(self.norm_two[0])) * self.wide(self.norm_two[1])
        return normed, normed * self.wide(self.gain_two[...])

    def conv_two(self):
        mean, inverse = self.norm_of(*self.wait_stats(1, self.local))
        self.norm_two[0], self.norm_two[1] = mean, inverse
        self.clear(2)

        def sweep(e):
            normed, scaled = self.second_norm(e)
            act, slope = silu_parts(scaled)
            put_shifted(self.stack_two, e, jnp.where(self.valid(e - 1), act, 0.0))
            grad = self.raw[e] * slope
            self.raw[e] = grad * self.wide(self.gain_two[...])
            mine = self.inside(e)
            self.acc[0, : self.local] += fold(grad) * mine
            self.acc[1, : self.local] += fold(grad * normed) * mine

        self.back.loop(self.rows + 2, self.ticks(2, 1), sweep)
        first, second = self.acc[0, : self.local], self.acc[1, : self.local]
        self.put_vec(1, second)
        gain = self.gain_two[...]
        self.send_stats(2, pack_sums([first * gain, second * gain]))
        for c in range(self.rows // self.step):

            self.conv_own(self.wt2, self.send_both, c * self.step, self.step)

            for copy in self.channel_copies(0, c):
                copy.start()

        self.weight_sum(self.cot, self.ticks(2, 0))
        for i in range(self.chans // 128):
            cols = slice(i * 128, (i + 1) * 128)
            self.put_taps(2 * self.index + 1, i, self.sums[:, cols].astype(BF16))

    def many_rows(self):
        return min(1024 // self.width, self.rows)

    def put_taps(self, which, block, values):
        if self.last is None:
            (self.gw1, self.gw2)[which % 2][which // 2, block] = values
        else:
            rows = values.shape[0]
            start = which * 9 * self.chans * self.local // 128 + block * rows
            self.taps[start : start + rows, :] = values

    def last_loop(self, count, ticks, body):
        if self.last is not None:
            self.last.loop(count, ticks, body)
        else:
            pl.loop(0, count)(body)

    def side_rows(self, y, together):
        side = [three_rows(self.stack_two, y + k) for k in range(together)]
        return jnp.concatenate(side, axis=1) if together > 1 else side[0]

    def conv_own(self, weights, target, start, count):
        together = self.row_pairs()

        def body(step):
            first = start + step * together
            product = dot(weights[...], self.side_rows(first, together)).astype(BF16)
            for k in range(together):
                target[first + k] = product[:, k * self.width : (k + 1) * self.width]

        self.back.loop(count // together, self.ticks(start // count % 2, start // count // 3), body)

    def put_vec(self, at, columns):
        lane = lax.broadcasted_iota(jnp.int32, (self.local, 128), 1)
        line = jnp.sum(columns, axis=1, keepdims=True)
        self.vec[...] = jnp.where(lane == at, line, self.vec[...])

    def channel_copies(self, which, c):
        out = self.send_both
        land = (self.got_two, self.got_one)[which]
        rows = pl.ds(c * self.step, self.step)
        copies = []
        for d in range(1, self.m):
            to = self.peer(d)
            chans = pl.ds(pl.multiple_of(to * self.local, self.local), self.local)
            copies.append(
                remote(
                    out.at[rows, chans, :],
                    land.at[d - 1, rows],
                    self.chan_send.at[self.index, which, d, c],
                    self.chan_recv.at[self.index, which, d, c],
                    {"mp": to},
                )
            )
        return copies

    def wait_channels(self, which):
        for c in range(self.rows // self.step):
            for copy in self.channel_copies(which, c):
                copy.wait_send()
                copy.wait_recv()

    def channel_sum(self, which, y):
        total = self.send_both[y, self.own, :].astype(F32)
        land = (self.got_two, self.got_one)[which]
        for d in range(1, self.m):
            total = total + land[d - 1, y].astype(F32)
        return total

    def back_one(self):
        first, second = self.wait_stats(2, self.local)
        self.norm_two[2], self.norm_two[3] = first / self.count, second / self.count
        self.acc[2, : self.local] = jnp.zeros((self.local, 128), F32)

        def sweep(e):
            normed, _ = self.second_norm(e)
            grad = self.raw[e] - self.wide(self.norm_two[2]) - normed * self.wide(self.norm_two[3])
            grad = jnp.where(self.valid(e - 1), grad * self.wide(self.norm_two[1]), 0.0)
            put_shifted(self.stack_two, e, grad)
            self.acc[2, : self.local] += fold(grad) * self.inside(e)

        self.back.loop(self.rows + 2, self.ticks(2, 1), sweep)
        self.put_vec(2, self.acc[2, : self.local])
        self.finish_out()
        for c in range(self.rows // self.step):

            self.conv_own(self.wb1, self.send_both, c * self.step, self.step)

            for copy in self.channel_copies(1, c):
                copy.start()

    def grad_weight_one(self):
        self.weight_sum(self.act, self.ticks(2, 0))
        for tap in range(9):
            rows = slice((8 - tap) * self.local, (9 - tap) * self.local)
            self.put_taps(2 * self.index, tap, self.sums[rows, :].T.astype(BF16))

    def weight_sum(self, source, ticks):
        together = self.many_rows()
        self.sums[...] = jnp.zeros(self.sums.shape, F32)

        def body(step):
            first = step * together
            block = jnp.concatenate([source[first + k + 2] for k in range(together)], axis=1)
            self.sums[...] += dot_nt(self.side_rows(first, together), block)

        self.back.loop(self.rows // together, ticks, body)

    def own_norm(self, y):
        mean, inverse = self.norm_one[0, self.own, :], self.norm_one[1, self.own, :]
        values = self.feats[y + 2, self.own, :].astype(F32)
        normed = (values - self.wide(mean)) * self.wide(inverse)
        return values, normed, inverse

    def last_sums(self):
        self.wait_channels(1)
        self.clear(2)

        def sweep(y):
            _, normed, _ = self.own_norm(y)
            _, slope = silu_parts(normed * self.wide(self.gain_one[...]))
            grad = self.channel_sum(1, y) * slope
            self.grad[y] = grad
            self.acc[0, : self.local] += fold(grad)
            self.acc[1, : self.local] += fold(grad * normed)

        self.last_loop(self.rows, self.ticks(5, 2), sweep)
        first, second = self.acc[0, : self.local], self.acc[1, : self.local]
        self.put_vec(0, second)
        gain = self.gain_one[...]
        self.send_stats(3, pack_sums([first * gain, second * gain]))

    def finish_out(self):
        self.wait_channels(0)

        @pl.loop(0, self.rows)
        def _(y):
            values = self.feats[y + 2, self.own, :].astype(F32)
            self.out[y] = (values + self.channel_sum(0, y)).astype(BF16)

    def finish_grad(self):
        first, second = self.wait_stats(3, self.local)
        self.norm_two[2], self.norm_two[3] = first / self.count, second / self.count

        def sweep(y):
            _, normed, inverse = self.own_norm(y)
            grad = self.grad[y] * self.wide(self.gain_one[...])
            grad = grad - self.wide(self.norm_two[2]) - normed * self.wide(self.norm_two[3])
            cot = self.cot[y + 2, self.own, :].astype(F32)
            self.grad[y] = cot + grad * self.wide(inverse)

        self.last_loop(self.rows, self.ticks(5, 2), sweep)


def conv_kernel(n, m, split, packable, *refs):
    refs = list(refs)

    def take(count):
        taken = refs[:count]
        del refs[:count]
        return taken

    own, gain_ref = take(2)
    sources, inputs = [], []
    for _ in range(2):
        sources.append((take(m), take(m)))
        inputs.append(take(len(ConvMap.INPUTS)))
    outputs = [take(len(ConvMap.OUTPUTS)) for _ in range(2)]
    vec_ref, gain_out, done = take(3)
    shared = {"last": None}
    if packable:
        last_done = take(1)[0]
    else:
        shared.update(zip(("gw1", "gw2"), take(2)))
    scratch = [take(len(ConvMap.SCRATCH)) for _ in range(2)]
    names = (
        "stat",
        "load_sem",
        "gain_send",
        "gain_recv",
        "edge_send",
        "edge_recv",
        "stat_send",
        "stat_recv",
        "chan_send",
        "chan_recv",
        "sums",
    )
    shared.update(zip(names, take(len(names))))
    piece = done.shape[0] // (RINGS * n)
    back = RingSum(n, piece, True, own, done, take(len(RingSum.SCRATCH)), split)
    shared["back"] = back
    last = None
    if packable:
        taps = take(1)[0]
        piece = taps.shape[0] // (RINGS * n)
        last = RingSum(n, piece, False, taps, last_done, take(len(RingSum.SCRATCH)))
        shared.update(taps=taps, last=last)
    maps = []
    for i in range(2):
        named = dict(zip(ConvMap.INPUTS, inputs[i]))
        named.update(zip(ConvMap.OUTPUTS, outputs[i]))
        named.update(zip(ConvMap.SCRATCH, scratch[i]))
        maps.append(ConvMap(i, n, m, sources[i], named, shared))

    for one in maps:
        for which in range(2):
            for copy in one.loads(which):
                copy.start()
    me, here = maps[0].me, maps[0].here
    greet(
        [{"seq": lax.rem(me + d, n)} for d in range(1, n)]
        + [{"mp": lax.rem(here + d, m)} for d in range(1, m)]
    )
    for one in maps:
        one.gains[one.own, :] = one.gain_one[...]
        one.vec[...] = jnp.zeros(one.vec.shape, F32)
        for copy in one.gain_copies():
            copy.start()
    for which in (1, 0):
        for one in maps:
            for copy in one.loads(which):
                copy.wait()
            one.start_edges(which)
    back.start()
    maps[1].send_stats(5, gain_ref[...])
    for one in maps:
        one.lay_out_weights()
    for one in maps:
        one.first_sums()
    back.first()
    for one in maps:
        one.wait_edges(1)
        one.back_two()
    for one in maps:
        for copy in one.gain_copies():
            copy.wait_send()
            copy.wait_recv()
        one.wait_edges(0)
        one.conv_one()
    for one in maps:
        one.conv_two()
    for one in maps:
        one.back_one()
    for one in maps:
        one.grad_weight_one()
    back.idle(back.ticks_all)
    if packable:
        rows = 4 * 9 * maps[0].chans * maps[0].local // 128
        if rows < taps.shape[0]:
            taps[rows:, :] = jnp.zeros((taps.shape[0] - rows, 128), BF16)
        last.start()
        last.first()
    for one in maps:
        one.last_sums()
    lines = [one.vec[...].T[:3] for one in maps]
    lines = jnp.concatenate(lines + [jnp.zeros((2, maps[0].local), F32)], axis=0)
    if maps[0].local < 128:
        blank = jnp.zeros((8, 128 - maps[0].local), F32)
        lines = jnp.concatenate([lines, blank], axis=1)
    maps[1].send_stats(4, lines)
    for one in maps:
        one.finish_grad()
    vec_ref[...] = maps[1].sum_stats(4)
    gain_out[...] = maps[1].sum_stats(5)
    back.finish()
    if packable:
        last.finish()


def res_blocks(maps, features, packed, vector, split, peers, n, m):
    args, in_any, outs, scratch = [packed, vector.reshape(8, 128)], [0], [], []
    for feats, cot, gain_one, conv_one, time_weight, gain_two, conv_two in maps:
        _, rows, local, width = feats.shape
        chans = conv_one.shape[2]
        for values in (feats[0], cot[0]):
            in_any += range(len(args), len(args) + m)
            args.append(values)
            args += peers.pop(0)
        shift = jnp.dot(features, time_weight.astype(F32), precision=HIGHEST)[0]
        args += [
            jnp.broadcast_to(column[:, None], (local, 128))
            for column in (gain_one, gain_two, shift)
        ]
        args += [conv_one, conv_two]
        outs += [
            ((rows, local, width), BF16),
            ((rows, local, width), F32),
        ]
        scratch += [
            pltpu.VMEM((rows + 4, chans, width), BF16),
            pltpu.VMEM((rows + 4, chans, width), BF16),
            pltpu.VMEM((rows + 4, chans, width), BF16),
            pltpu.VMEM((rows + 2, 3, local, width), BF16),
            pltpu.VMEM((3 * local, 3 * chans), BF16),
            pltpu.VMEM((chans, 9 * local), BF16),
            pltpu.VMEM((3 * local, 3 * chans), BF16),
            pltpu.VMEM((chans, 9 * local), BF16),
            pltpu.VMEM((rows + 2, local, width), F32),
            pltpu.VMEM((rows + 2, local, width), F32),
            pltpu.VMEM((rows, chans, width), BF16),
            pltpu.VMEM((m - 1, rows, local, width), BF16),
            pltpu.VMEM((m - 1, rows, local, width), BF16),
            pltpu.VMEM((chans, 128), F32),
            pltpu.VMEM((4, chans, 128), F32),
            pltpu.VMEM((4, local, 128), F32),
            pltpu.VMEM((3, chans, 128), F32),
            pltpu.VMEM((local, 128), F32),
        ]
    dma = pltpu.SemaphoreType.DMA
    rest = packed.shape[0] - split
    scratch += [
        pltpu.VMEM((10, n, 8, 128), F32),
        dma((2, 2, m)),
        dma((2, m)),
        dma((2, m)),
        dma((2, 2, 2)),
        dma((2, 2, 2)),
        dma((10,)),
        dma((10,)),
        dma((2, 2, m, 4)),
        dma((2, 2, m, 4)),
        pltpu.VMEM((9 * local, chans), F32),
    ] + RingSum.scratch(n, rest // (RINGS * n), True)
    outs += [((8, 128), F32), ((8, 128), F32), ((rest, 128), BF16)]
    out_any = [len(outs) - 1]
    packable = local % 128 == 0
    block = 9 * chans * local // 128
    if packable:
        grain = RINGS * n * 16
        taps = -(-4 * block // grain) * grain
        scratch += [pltpu.VMEM((taps, 128), BF16)]
        scratch += RingSum.scratch(n, taps // (RINGS * n), False)
        out_any.append(len(outs))
        outs.append(((taps, 128), BF16))
    else:
        outs += [
            ((2, 9, chans, local), BF16),
            ((2, chans // 128, 9 * local, 128), BF16),
        ]
    kernel = partial(conv_kernel, n, m, split, packable)
    results = vmem_call(kernel, outs, scratch, 4, "res_blocks", in_any, out_any)(*args)
    if packable:
        parts = [results[-1][at * block : (at + 1) * block] for at in range(4)]
        ones, twos = parts[::2], parts[1::2]
    else:
        ones, twos = lax.psum((results[-2], results[-1]), "seq")
    ones = [part.reshape(3, 3, chans, local).astype(F32) for part in ones]
    twos = [part.reshape(chans // 128, 3, 3, local, 128) for part in twos]
    twos = [jnp.concatenate(list(part), axis=-1).astype(F32) for part in twos]
    return results[:7], ones, twos


def text_grads(prompt, text):
    length, width = prompt.shape
    local = (text.shape[1] - 128) // 2
    block = 512

    def kernel(prompt_ref, text_ref, key_ref, value_ref):
        turned = turn(prompt_ref[...])
        key_ref[...] = dot(turned, text_ref[:, :local])
        value_ref[...] = dot(turned, text_ref[:, local : 2 * local])

    out = jax.ShapeDtypeStruct((width, local), F32)
    return pl.pallas_call(
        kernel,
        grid=(width // block,),
        in_specs=[
            pl.BlockSpec((length, block), lambda i: (0, i)),
            pl.BlockSpec(text.shape, lambda i: (0, 0)),
        ],
        out_specs=[pl.BlockSpec((block, local), lambda i: (i, 0))] * 2,
        out_shape=[out, out],
        compiler_params=pltpu.CompilerParams(vmem_limit_bytes=VMEM_LIMIT),
        name="text_grads",
    )(prompt, text)


def time_features(steps, width):
    half = width // 2
    freqs = jnp.exp(-math.log(10000.0) * jnp.arange(half, dtype=jnp.float32) / half)
    angles = steps.astype(jnp.float32)[:, None] * freqs[None, :]
    return jax.nn.silu(jnp.concatenate([jnp.cos(angles), jnp.sin(angles)], axis=1))


def on_device(
    tokens,
    prompt_embed,
    out_grad,
    norm_self,
    w_query,
    w_key,
    w_value,
    w_out,
    norm_cross,
    c_query,
    c_key,
    c_value,
    c_out,
    norm_feed,
    w_up,
    b_up,
    w_down,
    b_down,
    timesteps,
    crop_feats,
    crop_grad_in,
    crop_gain_one,
    crop_conv_one,
    crop_time,
    crop_gain_two,
    crop_conv_two,
    mid_feats,
    mid_grad_in,
    mid_gain_one,
    mid_conv_one,
    mid_time,
    mid_gain_two,
    mid_conv_two,
):
    n, m = lax.axis_size("seq"), lax.axis_size("mp")
    x = tokens[0]
    h1, qh, kv, log, ah, mix = attn_forward(
        x, norm_self[None], w_query, w_key, w_value, n
    )
    peers = []
    for values in (crop_feats, crop_grad_in, mid_feats, mid_grad_in):
        peers.append(
            [
                lax.ppermute(values[0], "mp", [((i + d) % m, i) for i in range(m)])
                for d in range(1, m)
            ]
        )
    mix, peers = lax.optimization_barrier((mix, peers))
    prompt = prompt_embed[0]
    keys_two = dot(prompt, c_key).astype(BF16)
    values_two = dot(prompt, c_value).astype(BF16)
    (
        base,
        units_sum,
        after,
        ga,
        text,
        packed,
    ) = middle(
        mix,
        x,
        out_grad[0],
        w_out,
        norm_cross[None],
        c_query,
        keys_two,
        values_two,
        c_out,
        norm_feed[None],
        w_up,
        b_up[None],
        w_down,
        b_down[None],
        n,
        m,
    )
    local_width = w_query.shape[1]
    features = time_features(timesteps, crop_time.shape[0])
    split = packed_split(local_width, w_up.shape[1], n)[0]
    grad_tokens, output, grad_norm_self, text_sum, packed, first_part = attn_backward(
        ga,
        qh,
        kv,
        log,
        ah,
        h1,
        x,
        norm_self[None],
        w_query,
        w_key,
        w_value,
        after,
        base,
        units_sum,
        text,
        packed,
        w_up.shape[1],
        n,
        m,
    )
    if text.shape[0] % (8 * n):
        text_sum = lax.psum(text, "seq").astype(BF16)
    grad_ckey, grad_cvalue = text_grads(prompt, text_sum)
    features = time_features(timesteps, crop_time.shape[0])
    (
        (crop_out, grad_crop, mid_out, grad_mid, conv_vec, norm_self_sum, second_part),
        (crop_cone, mid_cone),
        (crop_ctwo, mid_ctwo),
    ) = (
        res_blocks(
        (
            (
                crop_feats,
                crop_grad_in,
                crop_gain_one,
                crop_conv_one,
                crop_time,
                crop_gain_two,
                crop_conv_two,
            ),
            (
                mid_feats,
                mid_grad_in,
                mid_gain_one,
                mid_conv_one,
                mid_time,
                mid_gain_two,
                mid_conv_two,
            ),
        ),
        features,
        packed,
        grad_norm_self,
        split,
        peers,
        n,
        m,
    ))
    (
        grad_cquery,
        grad_cout,
        grad_out,
        grad_up,
        grad_down,
        grad_query,
        grad_key,
        grad_value,
    ) = unpack(first_part, second_part, local_width, w_up.shape[1])
    joined = text_sum[:, 2 * local_width :].astype(F32).reshape(-1)
    sizes = (D, D, w_up.shape[1], D)
    ends = [sum(sizes[: i + 1]) for i in range(len(sizes))]
    norm_cross_sum, norm_feed_sum, up_bias_sum, down_bias_sum = [
        joined[end - size : end] for size, end in zip(sizes, ends)
    ]
    norm_self_sum = norm_self_sum.reshape(-1)
    crop_gone, crop_gtwo, crop_hid, mid_gone, mid_gtwo, mid_hid = conv_vec[
        :6, : crop_gain_one.shape[0]
    ]

    def time_grad(sums):
        return features.T * sums[None, :]

    return (
        output[None],
        grad_tokens[None],
        norm_self_sum,
        grad_query,
        grad_key,
        grad_value,
        grad_out,
        norm_cross_sum,
        grad_cquery,
        grad_ckey,
        grad_cvalue,
        grad_cout,
        norm_feed_sum,
        grad_up,
        up_bias_sum,
        grad_down,
        down_bias_sum,
        crop_out[None],
        grad_crop[None],
        crop_gone,
        crop_cone,
        time_grad(crop_hid),
        crop_gtwo,
        crop_ctwo,
        mid_out[None],
        grad_mid[None],
        mid_gone,
        mid_cone,
        time_grad(mid_hid),
        mid_gtwo,
        mid_ctwo,
    )


def solution(mesh):
    in_specs = (
        P(None, "seq", None),
        P(),
        P(None, "seq", None),
        P(),
        P(None, "mp"),
        P(None, "mp"),
        P(None, "mp"),
        P("mp", None),
        P(),
        P(None, "mp"),
        P(None, "mp"),
        P(None, "mp"),
        P("mp", None),
        P(),
        P(None, "mp"),
        P("mp"),
        P("mp", None),
        P(),
        P(),
        P(None, "seq", "mp", None),
        P(None, "seq", "mp", None),
        P("mp"),
        P(None, None, None, "mp"),
        P(None, "mp"),
        P("mp"),
        P(None, None, "mp", None),
        P(None, "seq", "mp", None),
        P(None, "seq", "mp", None),
        P("mp"),
        P(None, None, None, "mp"),
        P(None, "mp"),
        P("mp"),
        P(None, None, "mp", None),
    )
    out_specs = (
        P(None, "seq", None),
        P(None, "seq", None),
        P(),
        P(None, "mp"),
        P(None, "mp"),
        P(None, "mp"),
        P("mp", None),
        P(),
        P(None, "mp"),
        P(None, "mp"),
        P(None, "mp"),
        P("mp", None),
        P(),
        P(None, "mp"),
        P("mp"),
        P("mp", None),
        P(),
        P(None, "seq", "mp", None),
        P(None, "seq", "mp", None),
        P("mp"),
        P(None, None, None, "mp"),
        P(None, "mp"),
        P("mp"),
        P(None, None, "mp", None),
        P(None, "seq", "mp", None),
        P(None, "seq", "mp", None),
        P("mp"),
        P(None, None, None, "mp"),
        P(None, "mp"),
        P("mp"),
        P(None, None, "mp", None),
    )
    return jax.shard_map(
        on_device, mesh=mesh, in_specs=in_specs, out_specs=out_specs, check_vma=False
    )
```

time: 1430 us -> 502 us (0.35)
  waiting for transfers between devices: 582 us -> 0.01 us
  Pallas kernels: 0 us -> 434 us
  matrix products: 251 us -> 6.53 us
  blocking collectives: 206 us -> 0 us
  local copies, waits for them, and re-layouts: 177 us -> 20.9 us
  other arithmetic: 139 us -> 24.4 us
  starting transfers between devices: 45.9 us -> 5.14 us
  between operations: 18 us -> 1.81 us
    psum x6 -> x0, waiting for transfers between devices: 515 us -> none  [the longest x1 400 us: on_device(): lax.psum(grad_ckey.astype(jnp.bfloat16), 'seq').astype(jnp.float32)]
    pallas_call x0 -> x5, Pallas kernels: none -> 434 us  [the longest x4 425 us: call(): pl.pallas_call(kernel, out_shape=[jax.ShapeDtypeStruct(shape, kind) for s...]
    dot_general x78 -> x4, matrix products: 218 us -> 6.53 us  [the longest x2 5.15 us: dot(): return jnp.dot(left, right, preferred_element_type=F32)]
    psum x5 -> x0, blocking collectives: 190 us -> none  [the longest x4 125 us: group_stats(): return lax.psum((first, second), 'seq')]
    unnamed x388 -> x51, local copies, waits for them, and re-layouts: 74.4 us -> 7.23 us
    all_gather x4 -> x0, waiting for transfers between devices: 65.9 us -> none  [the longest x1 50.1 us: on_device(): lax.all_gather(keys, 'seq', axis=1, tiled=True)]
    reduce_sum x37 -> x0, other arithmetic: 45.1 us -> none  [the longest x2 14.4 us: attend(): total = jnp.sum(expo, axis=-1, keepdims=True)]
    convert_element_type x28 -> x12, other arithmetic: 64.9 us -> 23.1 us  [the longest x7 18 us: unpack(): part.transpose(1, 0, 2).reshape(height, count * 128).astype(F32)]
  transfers between devices with their start and end apart: 32 -> 4, of which waited for: 8 -> 0; matrix products, arithmetic and copies ran while one was open for 32% -> 1% of each run, Pallas kernels for 0% -> 12%
where the time goes in v1:
time: 502 us; the launch traced here: 493 us
  Pallas kernels  434 us (86%)
  other arithmetic  24.4 us (5%)
  local copies, waits for them, and re-layouts  20.9 us (4%)
  matrix products  6.53 us (1%)
  starting transfers between devices  5.14 us (1%)
    pallas_call x4, Pallas kernels, call(): pl.pallas_call(kernel, out_shape=[jax.ShapeDtypeStruct(shape, kind) for s...  425 us
    convert_element_type x7, other arithmetic, unpack(): part.transpose(1, 0, 2).reshape(height, count * 128).astype(F32)  18 us
  transfers between devices with their start and end apart: 4, of which 0 were waited for; matrix products, arithmetic and copies ran while one was open for 1% of the time, Pallas kernels for 12%

profile of v1, /device:TPU:0, one launch (start us, length us, event | category | flops | bytes accessed | tf_op | source)
XLA Modules:
  0.0 492.7 jit_solution(3955676543144839640)
XLA Ops:
  0.7 3.0 collective-permute-start.2
  3.8 1.9 collective-permute-start
  6.6 59.0 %attn_forward.1 = (bf16[256,1024]{1,0:T(8,128)(2,1)}, bf16[64,2048]{1,0:T(8,128)(2,1)}, bf16[2,64,4096]{2,1,0:T(8,128)(2,1)}, f32[8,1,256]{2,1,0:T(1,128)}, f32[...) custom-call(bf16[256,1024]{1,0:T(8,128)(2,1)} %bitcast.132, f32[1,1024]{1,0:T(1,128)} %bitcast.164, bf16[1024,512]{1,0:T(8,128)(2,1)} %wq_ref.3, ...), custom_call_target="tpu_custom_call" | custom-call | tf_op jit(solution)/shard_map/attn_forward/pallas_call | solution.py:68
  65.8 1.2 convolution_bitcast_fusion.1
  66.9 3.7 convolution_convert_fusion.1.k2_ref
  70.7 1.4 convolution_convert_fusion.v2_ref
  72.2 58.0 %middle.1 = (f32[256,1024]{1,0:T(8,128)}, bf16[256,1024]{1,0:T(8,128)(2,1)}, f32[256,1024]{1,0:T(8,128)}, bf16[512,256]{1,0:T(8,128)(2,1)}, f32[128,1152]{1,0:T(8,128)}, /*index=5*/bf16[57344,128]{1,0:T(8,128)(2,1)}) custom-call(bf16[512,256]{1,0:T(8,128)(2,1)} %get-tuple-element.65.mix_ref, bf16[256,1024]{1,0:T(8,128)(2,1)} %bitcast.133, ...), custom_call_target="tpu_custom_call" | custom-call | tf_op jit(solution)/shard_map/middle/pallas_call | solution.py:68
  130.3 109.1 %attn_backward.1 = (f32[256,1024]{1,0:T(8,128)}, bf16[256,1024]{1,0:T(8,128)(2,1)}, f32[1,1024]{1,0:T(1,128)}, bf16[128,1152]{1,0:T(8,128)(2,1)}, bf16[57344,128...) custom-call(bf16[512,256]{1,0:T(8,128)(2,1)} %get-tuple-element.66.ga_ref, ...), custom_call_target="tpu_custom_call", output_to_operand_aliasing={{4}: (15, {})} | custom-call | tf_op jit(solution)/shard_map/attn_backward/pallas_call | solution.py:68
  239.3 0.8 slice_convert_fusion
  242.7 0.7 broadcast_in_dim.77.refs_6_
  245.6 199.2 %res_blocks.1 = (bf16[16,128,256]{2,1,0:T(8,128)(2,1)}, f32[16,128,256]{2,1,0:T(8,128)}, bf16[8,128,128]{2,1,0:T(8,128)(2,1)}, f32[8,128,128]{2,1,0:T(8,128)}, f...) custom-call(bf16[57344,128]{1,0:T(8,128)(2,1)} %get-tuple-element.79.refs_0_, ...), custom_call_target="tpu_custom_call" | custom-call | tf_op jit(solution)/shard_map/res_blocks/pallas_call | solution.py:68
  444.8 1.5 fusion.7
  446.9 2.1 fusion.5
  448.9 3.9 fusion.4
  453.5 1.6 copy_bitcast_fusion.3
  455.6 1.1 convert.34
  456.7 1.1 convert.35
  457.8 1.6 copy_bitcast_fusion.6
  459.4 1.6 copy_bitcast_fusion.5
  461.0 1.6 copy_bitcast_fusion.7
  462.6 4.5 copy_bitcast_fusion.1
  467.1 4.5 copy_bitcast_fusion
  471.6 8.8 %text_grads.1 = (f32[4096,512]{1,0:T(8,128)}, f32[4096,512]{1,0:T(8,128)}) custom-call(bf16[128,4096]{1,0:T(8,128)(2,1)} %bitcast.131, bf16[128,1152]{1,0:T(8,128)(2,1)} %get-tuple-element.88.text_ref), custom_call_target="tpu_custom_call" | custom-call | tf_op jit(solution)/shard_map/text_grads/pallas_call | solution.py:1905
  480.4 2.6 copy_bitcast_fusion.2
  483.0 1.2 broadcast_multiply_fusion
  484.2 1.1 maximum_convert_fusion.1
  485.3 1.1 maximum_convert_fusion
  486.3 0.8 copy.98
  487.1 1.0 copy.99
  488.7 1.0 copy.101
  489.7 1.3 copy.102
  491.7 0.8 copy.104
  (65 shorter events, 8.4 us)
Async XLA Ops:
  0.7 64.9 %copy-start = (bf16[1024,128]{1,0:T(8,128)(2,1)S(1)}, bf16[1024,128]{1,0:T(8,128)(2,1)}, u32[]{:S(2)}) copy-start(bf16[1024,128]{1,0:T(8,128)(2,1)} %param.63) | copy-start | bytes 786436
  0.7 66.2 %copy-start.2 = (bf16[1,128,4096]{2,1,0:T(8,128)(2,1)S(1)}, bf16[1,128,4096]{2,1,0:T(8,128)(2,1)}, u32[]{:S(2)}) copy-start(bf16[1,128,4096]{2,1,0:T(8,128)(2,1)} %param.34) | copy-start | bytes 3145732
  0.7 71.4 %collective-permute-start.2 = (bf16[8,128,128]{2,1,0:T(8,128)(2,1)}, bf16[8,128,128]{2,1,0:T(8,128)(2,1)S(1)}, u32[]{:S(2)}, u32[]{:S(2)}) collective-permute-start(bf16[8,128,128]{2,1,0:T(8,128)(2,1)} %bitcast.157), channel_id=1, source_target_pairs={{1,0},{0,1},{3,2},{2,3},{5,4},{4,5},{7,6},{6,7},{9,8},{8,9},{11,10... | collective-permute-start | bytes 786440 | tf_op jit(solution)/shard_map/ppermute | solution.py:1970
  3.7 68.4 %collective-permute-start.3 = (bf16[8,128,128]{2,1,0:T(8,128)(2,1)}, bf16[8,128,128]{2,1,0:T(8,128)(2,1)S(1)}, u32[]{:S(2)}, u32[]{:S(2)}) collective-permute-start(bf16[8,128,128]{2,1,0:T(8,128)(2,1)} %bitcast.159), channel_id=1, source_target_pairs={{1,0},{0,1},{3,2},{2,3},{5,4},{4,5},{7,6},{6,7},{9,8},{8,9},{11,10... | collective-permute-start | bytes 786440 | tf_op jit(solution)/shard_map/ppermute | solution.py:1970
  3.8 68.3 %collective-permute-start = (bf16[16,128,256]{2,1,0:T(8,128)(2,1)}, bf16[16,128,256]{2,1,0:T(8,128)(2,1)S(1)}, u32[]{:S(2)}, u32[]{:S(2)}) collective-permute-start(bf16[16,128,256]{2,1,0:T(8,128)(2,1)} %bitcast.148), channel_id=1, source_target_pairs={{1,0},{0,1},{3,2},{2,3},{5,4},{4,5},{7,6},{6,7},{9,8},{8,9},{11,10... | collective-permute-start | bytes 3145736 | tf_op jit(solution)/shard_map/ppermute | solution.py:1970
  5.8 66.4 %collective-permute-start.1 = (bf16[16,128,256]{2,1,0:T(8,128)(2,1)}, bf16[16,128,256]{2,1,0:T(8,128)(2,1)S(1)}, u32[]{:S(2)}, u32[]{:S(2)}) collective-permute-start(bf16[16,128,256]{2,1,0:T(8,128)(2,1)} %bitcast.150), channel_id=1, source_target_pairs={{1,0},{0,1},{3,2},{2,3},{5,4},{4,5},{7,6},{6,7},{9,8},{8,9},{11,10... | collective-permute-start | bytes 3145736 | tf_op jit(solution)/shard_map/ppermute | solution.py:1970
  66.9 3.7 copy-start.3
  72.1 58.1 %copy-start.13 = (bf16[8,128,128]{2,1,0:T(8,128)(2,1)}, bf16[8,128,128]{2,1,0:T(8,128)(2,1)S(1)}, u32[]{:S(2)}) copy-start(bf16[8,128,128]{2,1,0:T(8,128)(2,1)S(1)} %collective-permute-done.2.refs_12_) | copy-start | bytes 786436
  72.1 58.1 %copy-start.14 = (bf16[8,128,128]{2,1,0:T(8,128)(2,1)}, bf16[8,128,128]{2,1,0:T(8,128)(2,1)S(1)}, u32[]{:S(2)}) copy-start(bf16[8,128,128]{2,1,0:T(8,128)(2,1)S(1)} %collective-permute-done.3.refs_14_) | copy-start | bytes 786436
  72.1 58.1 %copy-start.7 = (bf16[16,128,256]{2,1,0:T(8,128)(2,1)}, bf16[16,128,256]{2,1,0:T(8,128)(2,1)S(1)}, u32[]{:S(2)}) copy-start(bf16[16,128,256]{2,1,0:T(8,128)(2,1)S(1)} %collective-permute-done.refs_3_) | copy-start | bytes 3145732
  72.1 58.0 %copy-start.8 = (bf16[16,128,256]{2,1,0:T(8,128)(2,1)}, bf16[16,128,256]{2,1,0:T(8,128)(2,1)S(1)}, u32[]{:S(2)}) copy-start(bf16[16,128,256]{2,1,0:T(8,128)(2,1)S(1)} %collective-permute-done.1.refs_5_) | copy-start | bytes 3145732
  130.2 112.5 %copy-start.18 = (f32[128]{0:T(128)S(1)}, f32[128]{0:T(128)}, u32[]{:S(2)}) copy-start(f32[128]{0:T(128)} %param.54) | copy-start | bytes 1540
  130.2 113.2 %copy-start.19 = (f32[128]{0:T(128)S(1)}, f32[128]{0:T(128)}, u32[]{:S(2)}) copy-start(f32[128]{0:T(128)} %param.57) | copy-start | bytes 1540
  130.2 113.9 %copy-start.20 = (f32[128]{0:T(128)S(1)}, f32[128]{0:T(128)}, u32[]{:S(2)}) copy-start(f32[128]{0:T(128)} %param.61) | copy-start | bytes 1540
  130.2 114.6 %copy-start.21 = (f32[128]{0:T(128)S(1)}, f32[128]{0:T(128)}, u32[]{:S(2)}) copy-start(f32[128]{0:T(128)} %param.64) | copy-start | bytes 1540
  444.8 2.0 copy-start.5
  448.9 4.4 copy-start.4
  453.5 1.6 copy-start.17
  483.0 3.4 copy-start.11
  484.2 3.0 copy-start.9
  485.2 2.9 copy-start.16
  485.3 3.5 copy-start.10
  487.1 2.5 copy-start.6
  488.7 3.8 copy-start.1
  489.7 1.3 copy-start.15
  489.7 2.0 copy-start.12

commit v2 on v1

--- a/solution.py
+++ b/solution.py
@@ -1784,13 +1784,13 @@
         one.back_one()
     for one in maps:
         one.grad_weight_one()
-    back.idle(back.ticks_all)
     if packable:
         rows = 4 * 9 * maps[0].chans * maps[0].local // 128
         if rows < taps.shape[0]:
             taps[rows:, :] = jnp.zeros((taps.shape[0] - rows, 128), BF16)
         last.start()
         last.first()
+    back.idle(back.ticks_all)
     for one in maps:
         one.last_sums()
     lines = [one.vec[...].T[:3] for one in maps]
@@ -1894,7 +1894,7 @@
 def text_grads(prompt, text):
     length, width = prompt.shape
     local = (text.shape[1] - 128) // 2
-    block = 512
+    block = 1024
 
     def kernel(prompt_ref, text_ref, key_ref, value_ref):
         turned = turn(prompt_ref[...])

time: 502 us -> 501 us (level)
  no operation moved by 1% of the time
where the time goes in v2:
time: 501 us; the launch traced here: 491 us
  Pallas kernels  433 us (86%)
  other arithmetic  24.4 us (5%)
  local copies, waits for them, and re-layouts  20.9 us (4%)
  matrix products  6.53 us (1%)
  starting transfers between devices  5.14 us (1%)
    pallas_call x4, Pallas kernels, call(): pl.pallas_call(kernel, out_shape=[jax.ShapeDtypeStruct(shape, kind) for s...  425 us
    convert_element_type x7, other arithmetic, unpack(): part.transpose(1, 0, 2).reshape(height, count * 128).astype(F32)  18 us
  transfers between devices with their start and end apart: 4, of which 0 were waited for; matrix products, arithmetic and copies ran while one was open for 1% of the time, Pallas kernels for 12%

profile of v2, /device:TPU:0, one launch (start us, length us, event | category | flops | bytes accessed | tf_op | source)
XLA Modules:
  0.0 491.4 jit_solution(13748175286219130119)
XLA Ops:
  0.7 3.0 collective-permute-start.2
  3.8 1.9 collective-permute-start
  6.6 59.0 %attn_forward.1 = (bf16[256,1024]{1,0:T(8,128)(2,1)}, bf16[64,2048]{1,0:T(8,128)(2,1)}, bf16[2,64,4096]{2,1,0:T(8,128)(2,1)}, f32[8,1,256]{2,1,0:T(1,128)}, f32[...) custom-call(bf16[256,1024]{1,0:T(8,128)(2,1)} %bitcast.132, f32[1,1024]{1,0:T(1,128)} %bitcast.164, bf16[1024,512]{1,0:T(8,128)(2,1)} %wq_ref.3, ...), custom_call_target="tpu_custom_call" | custom-call | tf_op jit(solution)/shard_map/attn_forward/pallas_call | solution.py:68
  65.8 1.2 convolution_bitcast_fusion.1
  66.9 3.7 convolution_convert_fusion.1.k2_ref
  70.7 1.4 convolution_convert_fusion.v2_ref
  72.2 58.0 %middle.1 = (f32[256,1024]{1,0:T(8,128)}, bf16[256,1024]{1,0:T(8,128)(2,1)}, f32[256,1024]{1,0:T(8,128)}, bf16[512,256]{1,0:T(8,128)(2,1)}, f32[128,1152]{1,0:T(8,128)}, /*index=5*/bf16[57344,128]{1,0:T(8,128)(2,1)}) custom-call(bf16[512,256]{1,0:T(8,128)(2,1)} %get-tuple-element.65.mix_ref, bf16[256,1024]{1,0:T(8,128)(2,1)} %bitcast.133, ...), custom_call_target="tpu_custom_call" | custom-call | tf_op jit(solution)/shard_map/middle/pallas_call | solution.py:68
  130.3 109.1 %attn_backward.1 = (f32[256,1024]{1,0:T(8,128)}, bf16[256,1024]{1,0:T(8,128)(2,1)}, f32[1,1024]{1,0:T(1,128)}, bf16[128,1152]{1,0:T(8,128)(2,1)}, bf16[57344,128...) custom-call(bf16[512,256]{1,0:T(8,128)(2,1)} %get-tuple-element.66.ga_ref, ...), custom_call_target="tpu_custom_call", output_to_operand_aliasing={{4}: (15, {})} | custom-call | tf_op jit(solution)/shard_map/attn_backward/pallas_call | solution.py:68
  239.3 0.8 slice_convert_fusion
  243.4 0.7 broadcast_in_dim.78.refs_7_
  245.6 199.2 %res_blocks.1 = (bf16[16,128,256]{2,1,0:T(8,128)(2,1)}, f32[16,128,256]{2,1,0:T(8,128)}, bf16[8,128,128]{2,1,0:T(8,128)(2,1)}, f32[8,128,128]{2,1,0:T(8,128)}, f...) custom-call(bf16[57344,128]{1,0:T(8,128)(2,1)} %get-tuple-element.79.refs_0_, ...), custom_call_target="tpu_custom_call" | custom-call | tf_op jit(solution)/shard_map/res_blocks/pallas_call | solution.py:68
  444.8 1.5 fusion.7
  446.9 2.1 fusion.5
  448.9 3.9 fusion.4
  453.5 1.6 copy_bitcast_fusion.3
  455.6 1.1 convert.34
  456.7 1.1 convert.35
  457.8 1.6 copy_bitcast_fusion.6
  459.4 1.6 copy_bitcast_fusion.5
  461.0 1.6 copy_bitcast_fusion.7
  462.6 4.5 copy_bitcast_fusion.1
  467.1 4.5 copy_bitcast_fusion
  471.6 7.4 %text_grads.1 = (f32[4096,512]{1,0:T(8,128)}, f32[4096,512]{1,0:T(8,128)}) custom-call(bf16[128,4096]{1,0:T(8,128)(2,1)} %bitcast.131, bf16[128,1152]{1,0:T(8,128)(2,1)} %get-tuple-element.88.text_ref), custom_call_target="tpu_custom_call" | custom-call | tf_op jit(solution)/shard_map/text_grads/pallas_call | solution.py:1905
  479.0 2.6 copy_bitcast_fusion.2
  481.6 1.2 broadcast_multiply_fusion
  482.8 1.1 maximum_convert_fusion.1
  483.9 1.1 maximum_convert_fusion
  485.0 0.8 copy.98
  485.8 1.0 copy.99
  487.3 1.0 copy.101
  488.3 1.3 copy.102
  490.3 0.8 copy.104
  (65 shorter events, 8.4 us)
Async XLA Ops:
  0.7 64.9 %copy-start = (bf16[1024,128]{1,0:T(8,128)(2,1)S(1)}, bf16[1024,128]{1,0:T(8,128)(2,1)}, u32[]{:S(2)}) copy-start(bf16[1024,128]{1,0:T(8,128)(2,1)} %param.63) | copy-start | bytes 786436
  0.7 66.2 %copy-start.2 = (bf16[1,128,4096]{2,1,0:T(8,128)(2,1)S(1)}, bf16[1,128,4096]{2,1,0:T(8,128)(2,1)}, u32[]{:S(2)}) copy-start(bf16[1,128,4096]{2,1,0:T(8,128)(2,1)} %param.34) | copy-start | bytes 3145732
  0.7 71.4 %collective-permute-start.2 = (bf16[8,128,128]{2,1,0:T(8,128)(2,1)}, bf16[8,128,128]{2,1,0:T(8,128)(2,1)S(1)}, u32[]{:S(2)}, u32[]{:S(2)}) collective-permute-start(bf16[8,128,128]{2,1,0:T(8,128)(2,1)} %bitcast.157), channel_id=1, source_target_pairs={{1,0},{0,1},{3,2},{2,3},{5,4},{4,5},{7,6},{6,7},{9,8},{8,9},{11,10... | collective-permute-start | bytes 786440 | tf_op jit(solution)/shard_map/ppermute | solution.py:1970
  3.7 68.4 %collective-permute-start.3 = (bf16[8,128,128]{2,1,0:T(8,128)(2,1)}, bf16[8,128,128]{2,1,0:T(8,128)(2,1)S(1)}, u32[]{:S(2)}, u32[]{:S(2)}) collective-permute-start(bf16[8,128,128]{2,1,0:T(8,128)(2,1)} %bitcast.159), channel_id=1, source_target_pairs={{1,0},{0,1},{3,2},{2,3},{5,4},{4,5},{7,6},{6,7},{9,8},{8,9},{11,10... | collective-permute-start | bytes 786440 | tf_op jit(solution)/shard_map/ppermute | solution.py:1970
  3.8 68.3 %collective-permute-start = (bf16[16,128,256]{2,1,0:T(8,128)(2,1)}, bf16[16,128,256]{2,1,0:T(8,128)(2,1)S(1)}, u32[]{:S(2)}, u32[]{:S(2)}) collective-permute-start(bf16[16,128,256]{2,1,0:T(8,128)(2,1)} %bitcast.148), channel_id=1, source_target_pairs={{1,0},{0,1},{3,2},{2,3},{5,4},{4,5},{7,6},{6,7},{9,8},{8,9},{11,10... | collective-permute-start | bytes 3145736 | tf_op jit(solution)/shard_map/ppermute | solution.py:1970
  5.8 66.4 %collective-permute-start.1 = (bf16[16,128,256]{2,1,0:T(8,128)(2,1)}, bf16[16,128,256]{2,1,0:T(8,128)(2,1)S(1)}, u32[]{:S(2)}, u32[]{:S(2)}) collective-permute-start(bf16[16,128,256]{2,1,0:T(8,128)(2,1)} %bitcast.150), channel_id=1, source_target_pairs={{1,0},{0,1},{3,2},{2,3},{5,4},{4,5},{7,6},{6,7},{9,8},{8,9},{11,10... | collective-permute-start | bytes 3145736 | tf_op jit(solution)/shard_map/ppermute | solution.py:1970
  66.9 3.7 copy-start.3
  72.1 58.1 %copy-start.13 = (bf16[8,128,128]{2,1,0:T(8,128)(2,1)}, bf16[8,128,128]{2,1,0:T(8,128)(2,1)S(1)}, u32[]{:S(2)}) copy-start(bf16[8,128,128]{2,1,0:T(8,128)(2,1)S(1)} %collective-permute-done.2.refs_12_) | copy-start | bytes 786436
  72.1 58.1 %copy-start.14 = (bf16[8,128,128]{2,1,0:T(8,128)(2,1)}, bf16[8,128,128]{2,1,0:T(8,128)(2,1)S(1)}, u32[]{:S(2)}) copy-start(bf16[8,128,128]{2,1,0:T(8,128)(2,1)S(1)} %collective-permute-done.3.refs_14_) | copy-start | bytes 786436
  72.1 58.1 %copy-start.7 = (bf16[16,128,256]{2,1,0:T(8,128)(2,1)}, bf16[16,128,256]{2,1,0:T(8,128)(2,1)S(1)}, u32[]{:S(2)}) copy-start(bf16[16,128,256]{2,1,0:T(8,128)(2,1)S(1)} %collective-permute-done.refs_3_) | copy-start | bytes 3145732
  72.1 58.0 %copy-start.8 = (bf16[16,128,256]{2,1,0:T(8,128)(2,1)}, bf16[16,128,256]{2,1,0:T(8,128)(2,1)S(1)}, u32[]{:S(2)}) copy-start(bf16[16,128,256]{2,1,0:T(8,128)(2,1)S(1)} %collective-permute-done.1.refs_5_) | copy-start | bytes 3145732
  130.2 112.5 %copy-start.18 = (f32[128]{0:T(128)S(1)}, f32[128]{0:T(128)}, u32[]{:S(2)}) copy-start(f32[128]{0:T(128)} %param.54) | copy-start | bytes 1540
  130.2 113.2 %copy-start.19 = (f32[128]{0:T(128)S(1)}, f32[128]{0:T(128)}, u32[]{:S(2)}) copy-start(f32[128]{0:T(128)} %param.57) | copy-start | bytes 1540
  130.2 113.9 %copy-start.20 = (f32[128]{0:T(128)S(1)}, f32[128]{0:T(128)}, u32[]{:S(2)}) copy-start(f32[128]{0:T(128)} %param.61) | copy-start | bytes 1540
  130.2 114.6 %copy-start.21 = (f32[128]{0:T(128)S(1)}, f32[128]{0:T(128)}, u32[]{:S(2)}) copy-start(f32[128]{0:T(128)} %param.64) | copy-start | bytes 1540
  444.8 2.0 copy-start.5
  448.9 4.4 copy-start.4
  453.5 1.6 copy-start.17
  481.6 3.4 copy-start.11
  482.8 3.0 copy-start.9
  483.9 2.9 copy-start.16
  483.9 3.5 copy-start.10
  485.8 2.5 copy-start.6
  487.3 3.8 copy-start.1
  488.3 1.3 copy-start.15
  488.3 2.0 copy-start.12
